TPU v7x, 32 devices: a whole 2x2x4 slice. The times are simulated.
32 devices in a mesh: seq: 16 (over z, y, x), tp: 2 (over core).
Axes of the slice: x: 2, y: 2, z: 4, core: 2. Of those that a mesh axis runs over, the one named last changes fastest.
Arguments:
- tokens: bfloat16 [32768, 768], P(('seq', 'tp')), may hold values from -6 to 6
- glob_tokens: bfloat16 [512, 768], P(('seq', 'tp')), may hold values from -6 to 6
- w_query: bfloat16 [768, 768], P(None, 'tp'), may hold values from -0.21875 to 0.21875
- b_query: float32 [768], P('tp'), may hold values from -2.5 to 2.5
- w_key: bfloat16 [768, 768], P(None, 'tp'), may hold values from -0.21875 to 0.21875
- w_value: bfloat16 [768, 768], P(None, 'tp'), may hold values from -0.21875 to 0.21875
- b_value: float32 [768], P('tp'), may hold values from -2.5 to 2.5
- w_out: bfloat16 [768, 768], P('tp'), may hold values from -0.875 to 0.875
- b_out: float32 [768], replicated, may hold values from -1.5 to 1.5
- w_up: bfloat16 [768, 3072], P(None, 'tp'), may hold values from -0.21875 to 0.21875
- b_up: float32 [3072], P('tp'), may hold values from -2.5 to 2.5
- w_down: bfloat16 [3072, 768], P('tp'), may hold values from -0.109375 to 0.109375
- b_down: float32 [768], replicated, may hold values from -1.5 to 1.5
- gain_attn: float32 [768], replicated, may hold values from 0.5 to 1.5
- shift_attn: float32 [768], replicated, may hold values from -1 to 1
- gain_ffn: float32 [768], replicated, may hold values from 0.5 to 1.5
- shift_ffn: float32 [768], replicated, may hold values from -1 to 1
- doc_blocks: int32 [4], replicated, may hold values from 1 to 31, as said below
- doc_tail: int32 [4], replicated, may hold values from 1 to 512
- grad_tokens: bfloat16 [32768, 768], P(('seq', 'tp')), may hold values from -6 to 6
- grad_glob: bfloat16 [512, 768], P(('seq', 'tp')), may hold values from -6 to 6
Outputs:
- out_tokens: bfloat16 [32768, 768], P(('seq', 'tp'))
- out_glob: bfloat16 [512, 768], P(('seq', 'tp'))
- tokens_grad: float32 [32768, 768], P(('seq', 'tp'))
- glob_grad: float32 [512, 768], P(('seq', 'tp'))
- w_query_grad: float32 [768, 768], P(None, 'tp')
- b_query_grad: float32 [768], P('tp')
- w_key_grad: float32 [768, 768], P(None, 'tp')
- w_value_grad: float32 [768, 768], P(None, 'tp')
- b_value_grad: float32 [768], P('tp')
- w_out_grad: float32 [768, 768], P('tp')
- b_out_grad: float32 [768], replicated
- w_up_grad: float32 [768, 3072], P(None, 'tp')
- b_up_grad: float32 [3072], P('tp')
- w_down_grad: float32 [3072, 768], P('tp')
- b_down_grad: float32 [768], replicated
- gain_attn_grad: float32 [768], replicated
- shift_attn_grad: float32 [768], replicated
- gain_ffn_grad: float32 [768], replicated
- shift_ffn_grad: float32 [768], replicated
Inputs may be any that keep to these rules, and one draw needn't show every extreme that they name: `doc_blocks`: documents lie one after another in tokens; documents 2p and 2p + 1 together span exactly 32 blocks, and one of the two is shorter than 4 blocks, so the entries sum to 64. `doc_tail`: the positions of a document's last block at or past this count are padding.
All inputs are finite; a program needn't handle non-finite values.
Results may differ from a plain program's by a relative error of at most 0.015.
Values may be sent and summed in bfloat16 or wider, within the bound.
No kernel may reach another device: no remote copies, remote signals or barrier semaphores. Data moves between devices by JAX's collectives and lax.ppermute only.
A program may use at most 192 MiB of HBM per device.

v0:
```python
import jax
import jax.numpy as jnp
from jax import lax
from jax.sharding import PartitionSpec as P

HD = 64
BLOCK = 512
GLOB = 128


EPS = 1e-05
SCALE = 0.125


def from_partner(value, axis, stride):
    mask = 2**stride
    pairs = [(source, source ^ mask) for source in range(lax.axis_size(axis))]
    return lax.ppermute(value, axis, pairs)


def norm_rows(values, gain_vec, shift_vec):
    row_mean = jnp.mean(values, axis=-1, keepdims=True)
    centred = values - row_mean
    row_var = jnp.mean(centred * centred, axis=-1, keepdims=True)
    return centred * lax.rsqrt(row_var + EPS) * gain_vec + shift_vec


def exact_gelu(values):
    return jax.nn.gelu(values, approximate=False)


def mat_prod(left, right):
    return jnp.dot(left, right, preferred_element_type=jnp.float32)


def outer_sum(left, right):
    return jnp.einsum("rd,rw->dw", left, right, preferred_element_type=jnp.float32)


def back_prod(grad_rows, weight):
    return jnp.einsum("rw,dw->rd", grad_rows, weight, preferred_element_type=jnp.float32)


def scores_of(queries, key_rows):
    return jnp.einsum("rhe,khe->hrk", queries, key_rows, preferred_element_type=jnp.float32)


def weighted(prob_rows, value_rows):
    return jnp.einsum("hrk,khe->rhe", prob_rows, value_rows, preferred_element_type=jnp.float32)


def keyed_sum(grad_rows, queries):
    return jnp.einsum("hrk,rhe->khe", grad_rows, queries, preferred_element_type=jnp.float32)


def norm_back(values, gain_vec, shift_vec, cotangent):
    pullback = jax.vjp(norm_rows, values, gain_vec, shift_vec)[1]
    return pullback(cotangent)


def block_layout(doc_blocks, doc_tail, first_block, block_count, block_len):
    doc_ends = jnp.cumsum(doc_blocks)
    block_ids = first_block + jnp.arange(block_count, dtype=jnp.int32)
    doc_of = jnp.sum((block_ids[:, None] >= doc_ends[None, :]).astype(jnp.int32), axis=1)
    picked = doc_of[:, None] == jnp.arange(doc_ends.shape[0], dtype=jnp.int32)[None, :]
    last_end = jnp.sum(jnp.where(picked, doc_ends[None, :], 0), axis=1)
    tail_len = jnp.sum(jnp.where(picked, doc_tail[None, :], 0), axis=1)
    tail_all = jnp.where(block_ids == last_end - 1, tail_len, block_len)
    key_valid = jnp.arange(block_len, dtype=jnp.int32)[None, :] < tail_all[:, None]
    return (doc_of, key_valid)


def halve_group(current, group_pos, bit_count, send_fn):
    for bit in reversed(range(bit_count)):
        half = current.shape[0] // 2
        upper_side = group_pos >> bit & 1 == 1
        lower_rows = current[:half]
        upper_rows = current[half:]
        outgoing = jnp.where(upper_side, lower_rows, upper_rows)
        staying = jnp.where(upper_side, upper_rows, lower_rows)
        current = staying + send_fn(outgoing, bit)
    return current


def double_group(current, group_pos, bit_count, send_fn):
    for bit in range(bit_count):
        other = send_fn(current, bit)
        upper_side = group_pos >> bit & 1 == 1
        current = jnp.where(
            upper_side, jnp.concatenate([other, current], 0), jnp.concatenate([current, other], 0)
        )
    return current


def per_device(
    tokens,
    glob_tokens,
    w_query,
    b_query,
    w_key,
    w_value,
    b_value,
    w_out,
    b_out,
    w_up,
    b_up,
    w_down,
    b_down,
    gain_attn,
    shift_attn,
    gain_ffn,
    shift_ffn,
    doc_blocks,
    doc_tail,
    grad_tokens,
    grad_glob,
):
    lowtype = jnp.bfloat16
    heads_here = w_query.shape[1] // HD
    width_here = w_query.shape[1]
    doc_count = doc_blocks.shape[0]
    seq_pos = lax.axis_index("seq")
    token_in = tokens.astype(jnp.float32)
    glob_in = glob_tokens.astype(jnp.float32)
    pair_tok = tokens.shape[0] * lax.axis_size("tp")
    pair_glob = glob_tokens.shape[0] * lax.axis_size("tp")
    block_count = pair_tok // BLOCK
    group_size = 32 // block_count
    bit_count = group_size.bit_length() - 1
    group_idx = seq_pos // group_size
    group_pos = seq_pos % group_size
    group_first = group_idx * 2
    doc_of, key_valid = block_layout(
        doc_blocks, doc_tail, seq_pos * block_count, block_count, BLOCK
    )
    doc_hot = (doc_of[:, None] == jnp.arange(doc_count, dtype=jnp.int32)[None, :]).astype(
        jnp.float32
    )
    group_hot = lax.dynamic_slice_in_dim(doc_hot, group_first, 2, 1)
    glob_start = seq_pos * pair_glob
    glob_ids = glob_start + jnp.arange(pair_glob, dtype=jnp.int32)
    group_ids = group_first * GLOB + jnp.arange(2 * GLOB, dtype=jnp.int32)
    own_mask = (glob_ids // GLOB)[:, None] == (group_ids // GLOB)[None, :]

    def to_heads(values):
        return values.reshape(values.shape[0], heads_here, HD)

    def to_blocks(values):
        return values.reshape(block_count, BLOCK, heads_here, HD)

    def doc_rows(array_in, doc_num):
        return lax.dynamic_slice_in_dim(array_in, doc_num * GLOB, GLOB, 0)

    def group_doc(array_in, doc_num):
        return lax.dynamic_slice_in_dim(array_in, (doc_num - group_first) * GLOB, GLOB, 0)

    def by_group(parts):
        flat = parts.reshape(parts.shape[0], -1)
        summed = jnp.dot(group_hot.T, flat, precision=lax.Precision.HIGHEST)
        return summed.reshape(2 * GLOB, -1)

    def pair_gather(tok_part, glob_part):
        return (
            lax.all_gather(tok_part, "tp", axis=0, tiled=True),
            lax.all_gather(glob_part, "tp", axis=0, tiled=True),
        )

    def pair_sum(rows_all):
        return (
            lax.psum_scatter(
                rows_all[:pair_tok].astype(jnp.bfloat16), "tp", scatter_dimension=0, tiled=True
            ).astype(jnp.float32),
            lax.psum_scatter(
                rows_all[pair_tok:].astype(jnp.bfloat16), "tp", scatter_dimension=0, tiled=True
            ).astype(jnp.float32),
        )

    def send_rows(outgoing, bit):
        return from_partner(outgoing, "seq", bit)

    def attention_inputs():
        normed_tok = norm_rows(token_in, gain_attn, shift_attn).astype(lowtype)
        normed_glob = norm_rows(glob_in, gain_attn, shift_attn).astype(lowtype)
        hidden_tok, hidden_glob = pair_gather(normed_tok, normed_glob)
        hidden_all = jnp.concatenate([hidden_tok, hidden_glob], 0)
        query_all = ((mat_prod(hidden_all, w_query) + b_query) * SCALE).astype(lowtype)
        key_all = mat_prod(hidden_all, w_key).astype(lowtype)
        value_all = (mat_prod(hidden_all, w_value) + b_value).astype(lowtype)
        packed = jnp.concatenate(
            [query_all[pair_tok:], key_all[pair_tok:], value_all[pair_tok:]], 1
        )
        glob_all = double_group(packed, group_pos, bit_count, send_rows)
        return (hidden_all, query_all, key_all, value_all, glob_all)

    def split_views(query_all, key_all, value_all, glob_all):
        glob_query = to_heads(glob_all[:, :width_here])
        glob_key = to_heads(glob_all[:, width_here : 2 * width_here])
        glob_value = to_heads(glob_all[:, 2 * width_here :])
        return (
            glob_query,
            glob_key,
            glob_value,
            to_blocks(query_all[:pair_tok]),
            to_blocks(key_all[:pair_tok]),
            to_blocks(value_all[:pair_tok]),
            to_heads(query_all[pair_tok:]),
        )

    hidden_all, query_all, key_all, value_all, glob_all = attention_inputs()
    glob_query, glob_key, glob_value, query_blocks, key_blocks, value_blocks, own_query = (
        split_views(query_all, key_all, value_all, glob_all)
    )

    def local_forward(block_item):
        query_blk, key_blk, value_blk, valid_blk, doc_num = block_item
        key_cat = jnp.concatenate([key_blk, group_doc(glob_key, doc_num)], 0)
        value_cat = jnp.concatenate([value_blk, group_doc(glob_value, doc_num)], 0)
        mask_cat = jnp.concatenate([valid_blk, jnp.ones((GLOB,), dtype=bool)])
        exp_scores = jnp.where(mask_cat, jnp.exp(scores_of(query_blk, key_cat)), 0.0)
        totals = jnp.sum(exp_scores, axis=-1)
        prob_low = (exp_scores / totals[:, :, None]).astype(lowtype)
        glob_exp = jnp.where(
            valid_blk, jnp.exp(scores_of(group_doc(glob_query, doc_num), key_blk)), 0.0
        )
        return (weighted(prob_low, value_cat), totals, jnp.sum(glob_exp, axis=-1))

    out_blocks, tot_blocks, glob_parts = lax.map(
        local_forward, (query_blocks, key_blocks, value_blocks, key_valid, doc_of)
    )
    own_exp = jnp.where(own_mask, jnp.exp(scores_of(own_query, glob_key)), 0.0)
    parts = jnp.transpose(glob_parts, (0, 2, 1))
    flat = parts.reshape(parts.shape[0], -1)
    summed = jnp.dot(doc_hot.T, flat, precision=lax.Precision.HIGHEST)
    glob_part_tot = summed.reshape(doc_count * GLOB, -1)
    own_rows_tot = (
        lax.dynamic_slice_in_dim(glob_part_tot, glob_start, pair_glob, 0)
        + jnp.sum(own_exp, axis=-1).T
    )
    glob_part_tot = lax.dynamic_update_slice_in_dim(glob_part_tot, own_rows_tot, glob_start, 0)
    glob_total = lax.psum(glob_part_tot, "seq")

    def glob_forward(block_item):
        key_blk, value_blk, valid_blk, doc_num = block_item
        total_doc = doc_rows(glob_total, doc_num).T
        glob_exp = jnp.where(
            valid_blk, jnp.exp(scores_of(group_doc(glob_query, doc_num), key_blk)), 0.0
        )
        prob_low = (glob_exp / total_doc[:, :, None]).astype(lowtype)
        return weighted(prob_low, value_blk)

    glob_blocks = lax.map(glob_forward, (key_blocks, value_blocks, key_valid, doc_of))
    own_total = lax.dynamic_slice_in_dim(glob_total, glob_start, pair_glob, 0).T
    own_prob = own_exp / own_total[:, :, None]
    own_out = weighted(own_prob.astype(lowtype), glob_value).reshape(pair_glob, width_here)

    def send_out(outgoing, bit):
        return from_partner(outgoing.astype(jnp.bfloat16), "seq", bit).astype(outgoing.dtype)

    glob_out = halve_group(by_group(glob_blocks), group_pos, bit_count, send_out) + own_out
    attn_low = jnp.concatenate([out_blocks.reshape(pair_tok, width_here), glob_out], 0).astype(
        lowtype
    )
    branch_tok, branch_glob = pair_sum(mat_prod(attn_low, w_out))
    middle_tok = token_in + branch_tok + b_out
    middle_glob = glob_in + branch_glob + b_out

    def ffn_inputs():
        normed_tok = norm_rows(middle_tok, gain_ffn, shift_ffn).astype(lowtype)
        normed_glob = norm_rows(middle_glob, gain_ffn, shift_ffn).astype(lowtype)
        hidden_tok, hidden_glob = pair_gather(normed_tok, normed_glob)
        ffn_hidden = jnp.concatenate([hidden_tok, hidden_glob], 0)
        up_proj = mat_prod(ffn_hidden, w_up) + b_up
        return (ffn_hidden, up_proj, exact_gelu(up_proj).astype(lowtype))

    ffn_hidden, up_proj, active = ffn_inputs()
    down_tok, down_glob = pair_sum(mat_prod(active, w_down))
    out_tokens = (middle_tok + down_tok + b_down).astype(lowtype)
    out_glob = (middle_glob + down_glob + b_down).astype(lowtype)
    ffn_hidden, up_proj, active = ffn_inputs()
    dz_tok, dz_glob = pair_gather(grad_tokens, grad_glob)
    dz_all = jnp.concatenate([dz_tok, dz_glob], 0)
    b_down_grad = jnp.sum(grad_tokens.astype(jnp.float32), 0) + jnp.sum(
        grad_glob.astype(jnp.float32), 0
    )
    w_down_grad = outer_sum(active, dz_all)
    d_active = back_prod(dz_all, w_down)
    d_up = jax.vjp(exact_gelu, up_proj)[1](d_active)[0].astype(lowtype)
    b_up_grad = jnp.sum(d_up.astype(jnp.float32), 0)
    w_up_grad = outer_sum(ffn_hidden, d_up)
    w_up_grad, b_up_grad, w_down_grad = lax.psum((w_up_grad, b_up_grad, w_down_grad), "seq")
    d_norm_tok, d_norm_glob = pair_sum(back_prod(d_up, w_up))
    d_mid_tok, gain_ffn_tok, shift_ffn_tok = norm_back(middle_tok, gain_ffn, shift_ffn, d_norm_tok)
    d_mid_glob, gain_ffn_glob, shift_ffn_glob = norm_back(
        middle_glob, gain_ffn, shift_ffn, d_norm_glob
    )
    d_mid_tok = d_mid_tok + grad_tokens.astype(jnp.float32)
    d_mid_glob = d_mid_glob + grad_glob.astype(jnp.float32)
    d_branch_tok = d_mid_tok.astype(lowtype)
    d_branch_glob = d_mid_glob.astype(lowtype)
    b_out_grad = jnp.sum(d_branch_tok.astype(jnp.float32), 0) + jnp.sum(
        d_branch_glob.astype(jnp.float32), 0
    )
    gathered_tok, gathered_glob = pair_gather(d_branch_tok, d_branch_glob)
    d_branch_all = jnp.concatenate([gathered_tok, gathered_glob], 0)
    w_out_grad = outer_sum(attn_low, d_branch_all)
    d_attn = back_prod(d_branch_all, w_out).astype(lowtype)
    hidden_all, query_all, key_all, value_all, glob_all = attention_inputs()
    glob_query, glob_key, glob_value, query_blocks, key_blocks, value_blocks, own_query = (
        split_views(query_all, key_all, value_all, glob_all)
    )
    d_out_glob = d_attn[pair_tok:]
    own_dout = to_heads(d_out_glob)
    delta_glob = jnp.sum(to_heads(d_out_glob.astype(jnp.float32)) * to_heads(glob_out), axis=-1)

    def send_back(outgoing, bit):
        return from_partner(outgoing.astype(jnp.bfloat16), "seq", bit).astype(outgoing.dtype)

    back_rows = double_group(
        jnp.concatenate([d_out_glob.astype(jnp.float32), delta_glob], 1),
        group_pos,
        bit_count,
        send_back,
    )
    dglob_low = to_heads(back_rows[:, :width_here].astype(lowtype))
    delta_all = back_rows[:, width_here:]

    def local_backward(block_item):
        query_blk, key_blk, value_blk, valid_blk, doc_num, dout_blk, out_blk, totals = block_item
        query_doc = group_doc(glob_query, doc_num)
        key_doc = group_doc(glob_key, doc_num)
        value_doc = group_doc(glob_value, doc_num)
        dout_doc = group_doc(dglob_low, doc_num)
        delta_doc = group_doc(delta_all, doc_num).T
        total_doc = doc_rows(glob_total, doc_num).T
        key_cat = jnp.concatenate([key_blk, key_doc], 0)
        value_cat = jnp.concatenate([value_blk, value_doc], 0)
        mask_cat = jnp.concatenate([valid_blk, jnp.ones((GLOB,), dtype=bool)])
        prob_full = (
            jnp.where(mask_cat, jnp.exp(scores_of(query_blk, key_cat)), 0.0) / totals[:, :, None]
        )
        row_delta = jnp.sum(dout_blk.astype(jnp.float32) * out_blk, axis=-1).T
        dscore = (prob_full * (scores_of(dout_blk, value_cat) - row_delta[:, :, None])).astype(
            lowtype
        )
        dkey_cat = keyed_sum(dscore, query_blk)
        dvalue_cat = keyed_sum(prob_full.astype(lowtype), dout_blk)
        glob_prob = (
            jnp.where(valid_blk, jnp.exp(scores_of(query_doc, key_blk)), 0.0)
            / total_doc[:, :, None]
        )
        glob_dscore = (glob_prob * (scores_of(dout_doc, value_blk) - delta_doc[:, :, None])).astype(
            lowtype
        )
        dkey_blk = dkey_cat[:BLOCK] + keyed_sum(glob_dscore, query_doc)
        dvalue_blk = dvalue_cat[:BLOCK] + keyed_sum(glob_prob.astype(lowtype), dout_doc)
        return (
            weighted(dscore, key_cat),
            dkey_blk,
            dvalue_blk,
            weighted(glob_dscore, key_blk),
            dkey_cat[BLOCK:],
            dvalue_cat[BLOCK:],
        )

    dq_blocks, dk_blocks, dv_blocks, dq_docs, dk_docs, dv_docs = lax.map(
        local_backward,
        (
            query_blocks,
            key_blocks,
            value_blocks,
            key_valid,
            doc_of,
            to_blocks(d_attn[:pair_tok]),
            out_blocks,
            tot_blocks,
        ),
    )
    own_exp = jnp.where(own_mask, jnp.exp(scores_of(own_query, glob_key)), 0.0)
    own_prob = own_exp / own_total[:, :, None]
    own_dscore = (own_prob * (scores_of(own_dout, glob_value) - delta_glob.T[:, :, None])).astype(
        lowtype
    )
    own_dq = weighted(own_dscore, glob_key).reshape(pair_glob, width_here)
    own_dk = keyed_sum(own_dscore, own_query).reshape(2 * GLOB, width_here)
    own_dv = keyed_sum(own_prob.astype(lowtype), own_dout).reshape(2 * GLOB, width_here)

    def send_grads(outgoing, bit):
        return from_partner(outgoing.astype(jnp.bfloat16), "seq", bit).astype(outgoing.dtype)

    stacked = jnp.concatenate(
        [by_group(dq_docs), by_group(dk_docs) + own_dk, by_group(dv_docs) + own_dv], 1
    )
    summed_all = halve_group(stacked, group_pos, bit_count, send_grads)
    sum_dq = summed_all[:, :width_here]
    sum_dk = summed_all[:, width_here : 2 * width_here]
    sum_dv = summed_all[:, 2 * width_here :]
    d_query = jnp.concatenate([dq_blocks.reshape(pair_tok, width_here), sum_dq + own_dq], 0).astype(
        lowtype
    )
    d_pre = d_query * SCALE
    d_key = jnp.concatenate([dk_blocks.reshape(pair_tok, width_here), sum_dk], 0).astype(lowtype)
    d_value = jnp.concatenate([dv_blocks.reshape(pair_tok, width_here), sum_dv], 0).astype(lowtype)
    w_query_grad = outer_sum(hidden_all, d_pre)
    b_query_grad = jnp.sum(d_pre.astype(jnp.float32), 0)
    w_key_grad = outer_sum(hidden_all, d_key)
    w_value_grad = outer_sum(hidden_all, d_value)
    b_value_grad = jnp.sum(d_value.astype(jnp.float32), 0)
    d_hidden = back_prod(d_pre, w_query) + back_prod(d_key, w_key) + back_prod(d_value, w_value)
    d_hidden_tok, d_hidden_glob = pair_sum(d_hidden)
    d_in_tok, gain_attn_tok, shift_attn_tok = norm_back(
        token_in, gain_attn, shift_attn, d_hidden_tok
    )
    d_in_glob, gain_attn_glob, shift_attn_glob = norm_back(
        glob_in, gain_attn, shift_attn, d_hidden_glob
    )
    tokens_grad = d_mid_tok + d_in_tok
    glob_grad = d_mid_glob + d_in_glob
    w_query_grad, b_query_grad, w_key_grad, w_value_grad, b_value_grad, w_out_grad = lax.psum(
        (w_query_grad, b_query_grad, w_key_grad, w_value_grad, b_value_grad, w_out_grad), "seq"
    )
    gain_attn_grad, shift_attn_grad, gain_ffn_grad, shift_ffn_grad, b_out_grad, b_down_grad = (
        lax.psum(
            (
                gain_attn_tok + gain_attn_glob,
                shift_attn_tok + shift_attn_glob,
                gain_ffn_tok + gain_ffn_glob,
                shift_ffn_tok + shift_ffn_glob,
                b_out_grad,
                b_down_grad,
            ),
            ("seq", "tp"),
        )
    )
    return (
        out_tokens,
        out_glob,
        tokens_grad,
        glob_grad,
        w_query_grad,
        b_query_grad,
        w_key_grad,
        w_value_grad,
        b_value_grad,
        w_out_grad,
        b_out_grad,
        w_up_grad,
        b_up_grad,
        w_down_grad,
        b_down_grad,
        gain_attn_grad,
        shift_attn_grad,
        gain_ffn_grad,
        shift_ffn_grad,
    )


def solution(mesh):
    return jax.shard_map(
        per_device,
        mesh=mesh,
        in_specs=(
            P(("seq", "tp"), None),
            P(("seq", "tp"), None),
            P(None, "tp"),
            P("tp"),
            P(None, "tp"),
            P(None, "tp"),
            P("tp"),
            P("tp", None),
            P(),
            P(None, "tp"),
            P("tp"),
            P("tp", None),
            P(),
            P(),
            P(),
            P(),
            P(),
            P(),
            P(),
            P(("seq", "tp"), None),
            P(("seq", "tp"), None),
        ),
        out_specs=(
            P(("seq", "tp"), None),
            P(("seq", "tp"), None),
            P(("seq", "tp"), None),
            P(("seq", "tp"), None),
            P(None, "tp"),
            P("tp"),
            P(None, "tp"),
            P(None, "tp"),
            P("tp"),
            P("tp", None),
            P(),
            P(None, "tp"),
            P("tp"),
            P("tp", None),
            P(),
            P(),
            P(),
            P(),
            P(),
        ),
        check_vma=False,
    )
```

profile of v0, /device:TPU:0, one launch (start us, length us, event | category | flops | bytes accessed | tf_op | source)
XLA Modules:
  0.0 1082.0 jit_solution(10830310447443557510)
XLA Ops:
  17.8 11.4 %all-gather.5.cloned.1.call-done = bf16[2048,768]{1,0:T(8,128)(2,1)} async-done(((bf16[1024,768]{1,0:T(8,128)(2,1)}), bf16[2048,768]{1,0:T(8,128)(2,1)}) %all-gather.5.cloned.1.call-update) | async-done | bytes 3145744 | tf_op jit(solution)/shard_map/all_gather | solution.py:164
  46.9 3.4 collective-permute-done.1
  62.0 3.8 reshape.356
  65.8 2.9 copy.251
  71.3 3.8 reshape.360
  75.1 2.9 copy.252
  80.6 3.8 reshape.361
  84.4 2.9 copy.253
  88.0 37.7 %while.47 = (s32[]{:T(128)}, f32[4,512,6,64]{1,3,2,0:T(8,128)}, f32[4,6,512]{2,1,0:T(8,128)}, f32[4,6,128]{2,1,0:T(8,128)S(1)}, bf16[4,512,6,64]{1,3,2,0:T(8,128...) while((s32[]{:T(128)}, f32[4,512,6,64]{1,3,2,0:T(8,128)}, ...), condition=%wide.region_11.12_spmd.clone, body=%wide.region_8.11_spmd.sunk.clone | while | flops 566227200 | bytes 20417644 | solution.py:227
  93.3 3.0 fusion.309
  102.8 3.0 fusion.309
  112.2 3.0 fusion.309
  121.6 3.0 fusion.309
  127.8 78.5 %psum.112 = f32[512,6]{1,0:T(8,128)S(1)} all-reduce(f32[512,6]{1,0:T(8,128)S(1)} %constant_dynamic-update-slice_fusion.8), channel_id=1, replica_groups=mesh['seq'=16,'tp'=2] {'seq'}, use_global_device_ids=true, to_apply=%region_13.14 | all-reduce | flops 3072 | bytes 24576 | tf_op jit(solution)/shard_map/psum | solution.py:240
  207.8 20.4 %while.48 = (s32[]{:T(128)}, f32[4,128,6,64]{1,3,2,0:T(8,128)S(1)}, bf16[4,512,6,64]{1,3,2,0:T(8,128)(2,1)}, pred[4,512]{1,0:T(4,128)(4,1)S(1)}, s32[4]{0:T(128)...) while((s32[]{:T(128)}, f32[4,128,6,64]{1,3,2,0:T(8,128)S(1)}, ...), condition=%wide.region_15.16_spmd.clone, body=%wide.region_14.15_spmd.sunk.clone | while | flops 101842952 | bytes 1095393 | solution.py:251
  230.2 3.3 reshape.368
  237.1 3.9 collective-permute-done.3
  242.0 3.3 collective-permute-done.4
  251.5 3.4 convolution_convert_fusion.2
  260.8 6.5 reduce-scatter.9.cloned.1.call-done
  275.5 6.8 all-gather.9.cloned.1.call-done
  282.3 3.8 constant_dynamic-update-slice_fusion.5
  286.7 6.9 reduce-scatter.11.cloned.1.call-done
  299.1 9.9 all-gather.7.cloned.1.call-done
  311.2 36.5 %multiply_convert_fusion.2 = (bf16[2080,1536]{1,0:T(8,128)(2,1)}, f32[2080,1536]{1,0:T(8,128)}, f32[2080,1536]{1,0:T(8,128)}) fusion(f32[1536]{0:T(1024)S(1)} %copy-done.138, bf16[2080,768]{1,0:T(8,128)(2,1)S(1)} %constant_dynamic-update-slice_fusion.2, bf16[768,1536]{1,0:T(8,128)(2,1)S(1)} %copy-done), kind=kOutput, calls=%fused_computation.114 | convolution fusion | flops 5118197760 | bytes 37509120 | tf_op jit(solution)/shard_map/dot_general | solution.py:33
  347.7 17.5 %convert_reduce_fusion = (f32[1536]{0:T(1024)}, bf16[2080,1536]{1,0:T(8,128)(2,1)}) fusion(f32[2080,1536]{1,0:T(8,128)} %get-tuple-element.660, f32[2080,1536]{1,0:T(8,128)} %get-tuple-element.693, bf16[2080,768]{1,0:T(8,128)(2,1)} %constant_dynamic-update-slice_fusion.4, bf16[1536,768]{1,0:T(8,128)(2,1)S(1)} %copy-done.135), kind=kOutput, calls=%fused_computation.112 | convolution fusion | flops 4958452224 | bytes 37509120 | tf_op jit(solution)/shard_map/rw,dw->rd/dot_general | solution.py:41
  365.2 8.4 convolution_convert_fusion
  378.8 8.3 convolution_convert_fusion.1
  394.0 3.9 fusion.104
  397.9 5.9 reduce-scatter.13.cloned.1.call-done
  403.7 4.6 fusion.173
  419.3 7.4 reduce-scatter.15.cloned.1.call-done
  430.9 11.2 %all-gather.11.cloned.1.call-done = bf16[2048,768]{1,0:T(8,128)(2,1)} async-done(((bf16[1024,768]{1,0:T(8,128)(2,1)}), bf16[2048,768]{1,0:T(8,128)(2,1)}) %all-gather.11.cloned.1.call-update) | async-done | bytes 3145744 | tf_op jit(solution)/shard_map/all_gather | solution.py:164
  460.8 2.9 reshape.370
  470.3 107.4 %while.49 = (s32[]{:T(128)}, bf16[4,512,6,64]{1,3,2,0:T(8,128)(2,1)}, bf16[4,512,6,64]{1,3,2,0:T(8,128)(2,1)}, bf16[4,512,6,64]{1,3,2,0:T(8,128)(2,1)}, f32[4,12...) while((s32[]{:T(128)}, ...), condition=%wide.region_33.34_spmd.clone, body=%wide.region_31.33_spmd.sunk.clone | while | flops 1528034304 | bytes 176738176 | solution.py:365
  595.0 6.4 collective-permute-done.9
  603.1 3.7 collective-permute-done.10
  626.5 3.8 slice.218
  630.3 10.3 fusion.184
  640.6 11.3 %fusion.185 = f32[1536,768]{1,0:T(8,128)} fusion(bf16[2080,1536]{1,0:T(8,128)(2,1)} %get-tuple-element.659, bf16[2080,768]{1,0:T(8,128)(2,1)} %constant_dynamic-update-slice_fusion.4), kind=kOutput, calls=%fused_computation.347 | convolution fusion | flops 4907335680 | bytes 14303232 | tf_op jit(solution)/shard_map/rd,rw->dw/dot_general | solution.py:37
  654.5 3.0 fusion.113
  657.5 3.0 fusion.116
  660.5 3.0 fusion.120
  667.8 78.8 %all-reduce.3 = (f32[384]{0:T(512)}, f32[384]{0:T(512)}, f32[1536]{0:T(1024)}) all-reduce(f32[384]{0:T(512)S(1)} %convert_reduce_fusion.6, f32[384]{0:T(512)S(1)} %convert_reduce_fusion.5, f32[1536]{0:T(1024)S(1)} %copy-done.121), channel_id=1, replica_groups=mesh['seq'=16,'tp'=2] {'seq'}, use_global_device_ids=true, to_apply=%region_42.43 | all-reduce | flops 2304 | bytes 18432 | tf_op jit(solution)/shard_map/psum | solution.py:418
  752.9 3.1 fusion.105
  756.0 2.8 convert_reduce_fusion.4
  758.9 41.3 %all-reduce.2 = (f32[768]{0:T(1024)}, f32[768]{0:T(1024)}, f32[768]{0:T(1024)}, f32[768]{0:T(1024)}, f32[768]{0:T(1024)}, /*index=5*/f32[768]{0:T(1024)}) all-reduce(f32[768]{0:T(1024)S(1)} %add.446, f32[768]{0:T(1024)S(1)} %add.447, f32[768]{0:T(1024)S(1)} %add.448, ...), channel_id=1, replica_groups=mesh['seq'=16,'tp'=2] {'seq','tp'}, use_global_device_ids=true, to_apply=%region_50.51 | all-reduce | flops 4608 | bytes 36864 | tf_op jit(solution)/shard_map/psum | solution.py:422
  800.2 264.2 %all-reduce.7.cloned.1.call-done = (f32[768,384]{1,0:T(8,128)}, f32[768,384]{1,0:T(8,128)}, f32[768,384]{1,0:T(8,128)}, f32[384,768]{1,0:T(8,128)}, f32[768,1536]{1,0:T(8,128)}, /*index=5*/f32[1536,768]{1,0:T(8,128)}) async-done(((f32[768,384]{1,0:T(8,128)}, f32[768,384]{1,0:T(8,128)}, f32[768,384]{1,0:T(8,128)}, f32[384,768]{1,0:T(8,128)}, f32[768,1536]{1,0:T(8,128)}, /*index=5*/f32[1536,768]{1,0:T(8,128)}), ...) | async-done | bytes 14155792 | tf_op jit(solution)/shard_map/psum | solution.py:418
  (723 shorter events, 337.0 us)
Async XLA Ops:
  7.2 304.0 %copy-start = (bf16[768,1536]{1,0:T(8,128)(2,1)S(1)}, bf16[768,1536]{1,0:T(8,128)(2,1)}, u32[]{:S(2)}) copy-start(bf16[768,1536]{1,0:T(8,128)(2,1)} %param.36) | copy-start | bytes 7077892
  7.2 22.0 %all-gather.5.cloned.1.call-start = ((), (), s32[]{:S(2)}) async-start(), calls=%async_computation.8 | async-start | bytes 4718592 | tf_op jit(solution)/shard_map/all_gather | solution.py:164
  14.2 253.2 %reduce-scatter.9.cloned.1.call-start = ((), (), s32[]{:S(2)}) async-start(), calls=%async_computation.9 | async-start | bytes 4718592 | tf_op jit(solution)/shard_map/reduce_scatter | solution.py:170
  40.4 4.5 collective-permute-start
  45.0 5.3 collective-permute-start.1
  46.8 186.7 %copy-start.117 = (pred[4,4]{1,0:T(4,128)(4,1)}, pred[4,4]{1,0:T(4,128)(4,1)S(1)}, u32[]{:S(2)}) copy-start(pred[4,4]{1,0:T(4,128)(4,1)S(1)} %iota_compare_fusion.1) | copy-start | bytes 52
  50.3 37.1 %collective-permute-start.2 = (bf16[128,1152]{1,0:T(8,128)(2,1)S(1)}, bf16[128,1152]{1,0:T(8,128)(2,1)S(1)}, u32[]{:S(2)}, u32[]{:S(2)}) collective-permute-start(bf16[128,1152]{1,0:T(8,128)(2,1)S(1)} %maximum_select_fusion.2), channel_id=1, source_target_pairs={{0,8},{2,10},{4,12},{6,14},{8,0},{10,2},{12,4},{14,6},{16,24},{18,... | collective-permute-start | bytes 884744 | tf_op jit(solution)/shard_map/ppermute | solution.py:18
  52.3 74.5 %copy-start.74 = (bf16[32,6,64]{2,1,0:T(8,128)(2,1)}, bf16[32,6,64]{2,1,0:T(8,128)(2,1)S(1)}, u32[]{:S(2)}) copy-start(bf16[32,6,64]{2,1,0:T(8,128)(2,1)S(1)} %reshape.367) | copy-start | bytes 73732
  125.8 80.6 %copy-start.47 = (bf16[256,6,64]{0,2,1:T(8,128)(2,1)}, bf16[256,6,64]{0,2,1:T(8,128)(2,1)S(1)}, u32[]{:S(2)}) copy-start(bf16[256,6,64]{0,2,1:T(8,128)(2,1)S(1)} %get-tuple-element.1313) | copy-start | bytes 589828
  125.8 82.1 %copy-start.20 = (bf16[256,6,64]{0,2,1:T(8,128)(2,1)}, bf16[256,6,64]{0,2,1:T(8,128)(2,1)S(1)}, u32[]{:S(2)}) copy-start(bf16[256,6,64]{0,2,1:T(8,128)(2,1)S(1)} %get-tuple-element.1293) | copy-start | bytes 589828
  125.8 119.6 %copy-start.22 = (bf16[256,6,64]{0,2,1:T(8,128)(2,1)}, bf16[256,6,64]{0,2,1:T(8,128)(2,1)S(1)}, u32[]{:S(2)}) copy-start(bf16[256,6,64]{0,2,1:T(8,128)(2,1)S(1)} %get-tuple-element.1295) | copy-start | bytes 589828
  236.4 4.7 collective-permute-start.3
  241.1 4.2 collective-permute-start.4
  245.3 5.4 collective-permute-start.5
  258.5 23.8 %all-gather.9.cloned.1.call-start = ((), (), s32[]{:S(2)}) async-start(), calls=%async_computation.14 | async-start | bytes 4718592 | tf_op jit(solution)/shard_map/all_gather | solution.py:164
  259.3 34.4 %reduce-scatter.11.cloned.1.call-start = ((), (), s32[]{:S(2)}) async-start(), calls=%async_computation.11 | async-start | bytes 73728 | tf_op jit(solution)/shard_map/reduce_scatter | solution.py:173
  260.8 48.2 %all-gather.7.cloned.1.call-start = ((), (), s32[]{:S(2)}) async-start(), calls=%async_computation.10 | async-start | bytes 4718592 | tf_op jit(solution)/shard_map/all_gather | solution.py:164
  273.2 120.7 %reduce-scatter.17.cloned.1.call-start = ((), (), s32[]{:S(2)}) async-start(), calls=%async_computation.15 | async-start | bytes 4718592 | tf_op jit(solution)/shard_map/reduce_scatter | solution.py:170
  275.5 18.1 %copy-start.44 = (bf16[16,768]{1,0:T(8,128)(2,1)S(1)}, bf16[16,768]{1,0:T(8,128)(2,1)}, u32[]{:S(2)}) copy-start(bf16[16,768]{1,0:T(8,128)(2,1)} %param.28) | copy-start | bytes 73732
  294.5 16.6 %copy-start.119 = (f32[16]{0:T(128)}, f32[16]{0:T(128)S(1)}, u32[]{:S(2)}) copy-start(f32[16]{0:T(128)S(1)} %broadcast_multiply_fusion.2) | copy-start | bytes 196
  311.2 36.6 %copy-start.40 = (bf16[2080,768]{1,0:T(8,128)(2,1)}, bf16[2080,768]{1,0:T(8,128)(2,1)S(1)}, u32[]{:S(2)}) copy-start(bf16[2080,768]{1,0:T(8,128)(2,1)S(1)} %constant_dynamic-update-slice_fusion.2) | copy-start | bytes 9584644
  311.2 36.6 %copy-start.135 = (bf16[1536,768]{1,0:T(8,128)(2,1)S(1)}, bf16[1536,768]{1,0:T(8,128)(2,1)}, u32[]{:S(2)}) copy-start(bf16[1536,768]{1,0:T(8,128)(2,1)} %param.38) | copy-start | bytes 7077892
  377.2 26.6 %reduce-scatter.13.cloned.1.call-start = ((), (), s32[]{:S(2)}) async-start(), calls=%async_computation.12 | async-start | bytes 4718592 | tf_op jit(solution)/shard_map/reduce_scatter | solution.py:170
  390.8 27.1 %reduce-scatter.19.cloned.1.call-start = ((), (), s32[]{:S(2)}) async-start(), calls=%async_computation.17 | async-start | bytes 73728 | tf_op jit(solution)/shard_map/reduce_scatter | solution.py:173
  392.4 34.3 %reduce-scatter.15.cloned.1.call-start = ((), (), s32[]{:S(2)}) async-start(), calls=%async_computation.13 | async-start | bytes 73728 | tf_op jit(solution)/shard_map/reduce_scatter | solution.py:173
  393.9 48.2 %all-gather.11.cloned.1.call-start = ((), (), s32[]{:S(2)}) async-start(), calls=%async_computation.16 | async-start | bytes 4718592 | tf_op jit(solution)/shard_map/all_gather | solution.py:164
  411.0 335.7 %reduce-scatter.23.cloned.1.call-start = ((), (), s32[]{:S(2)}) async-start(), calls=%async_computation.19 | async-start | bytes 73728 | tf_op jit(solution)/shard_map/reduce_scatter | solution.py:173
  446.5 4.0 collective-permute-start.6
  450.5 4.3 collective-permute-start.7
  455.6 11.4 %collective-permute-start.8 = (bf16[128,390]{1,0:T(8,128)(2,1)}, bf16[128,390]{1,0:T(8,128)(2,1)S(1)}, u32[]{:S(2)}, u32[]{:S(2)}) collective-permute-start(bf16[128,390]{1,0:T(8,128)(2,1)} %get-tuple-element.651), channel_id=1, source_target_pairs={{0,8},{2,10},{4,12},{6,14},{8,0},{10,2},{12,4},{14,6},{16,24},{18,... | collective-permute-start | bytes 299528 | tf_op jit(solution)/shard_map/ppermute | solution.py:18
  594.7 6.8 collective-permute-start.9
  601.6 5.2 collective-permute-start.10
  606.9 10.9 %collective-permute-start.11 = (bf16[32,1152]{1,0:T(8,128)(2,1)S(1)}, bf16[32,1152]{1,0:T(8,128)(2,1)S(1)}, u32[]{:S(2)}, u32[]{:S(2)}) collective-permute-start(bf16[32,1152]{1,0:T(8,128)(2,1)S(1)} %select_convert_fusion.2), channel_id=1, source_target_pairs={{0,2},{2,0},{4,6},{6,4},{8,10},{10,8},{12,14},{14,12},{16,18},{18,... | collective-permute-start | bytes 221192 | tf_op jit(solution)/shard_map/ppermute | solution.py:18
  611.9 48.5 %copy-start.13 = (bf16[48,8,4,512]{3,1,2,0:T(8,128)(2,1)}, bf16[48,8,4,512]{3,1,2,0:T(8,128)(2,1)S(1)}, u32[]{:S(2)}) copy-start(bf16[48,8,4,512]{3,1,2,0:T(8,128)(2,1)S(1)} %copy.292) | copy-start | bytes 4718596
  626.4 123.6 %reduce-scatter.21.cloned.1.call-start = ((), (), s32[]{:S(2)}) async-start(), calls=%async_computation.18 | async-start | bytes 4718592 | tf_op jit(solution)/shard_map/reduce_scatter | solution.py:170
  630.2 434.1 %all-reduce.7.cloned.1.call-start = ((), (), s32[]{:S(2)}) async-start(), calls=%async_computation.20 | async-start | bytes 28311552 | tf_op jit(solution)/shard_map/psum | solution.py:418
  663.6 83.1 %copy-start.46 = (bf16[16,768]{1,0:T(8,128)(2,1)S(1)}, bf16[16,768]{1,0:T(8,128)(2,1)}, u32[]{:S(2)}) copy-start(bf16[16,768]{1,0:T(8,128)(2,1)} %param.28) | copy-start | bytes 73732
  663.6 83.1 %copy-start.81 = (f32[768]{0:T(1024)S(1)}, f32[768]{0:T(1024)}, u32[]{:S(2)}) copy-start(f32[768]{0:T(1024)} %param.40) | copy-start | bytes 9220
  663.6 83.1 %copy-start.116 = (f32[16]{0:T(128)S(1)}, f32[16]{0:T(128)}, u32[]{:S(2)}) copy-start(f32[16]{0:T(128)} %copy-done.115) | copy-start | bytes 196
  663.6 84.0 %copy-start.132 = (f32[16]{0:T(128)S(1)}, f32[16]{0:T(128)}, u32[]{:S(2)}) copy-start(f32[16]{0:T(128)} %copy-done.131) | copy-start | bytes 196
  663.6 84.0 %copy-start.125 = (f32[16]{0:T(128)S(1)}, f32[16]{0:T(128)}, u32[]{:S(2)}) copy-start(f32[16]{0:T(128)} %copy-done.124) | copy-start | bytes 196
  663.6 85.0 %copy-start.73 = (f32[16,768]{1,0:T(8,128)S(1)}, f32[16,768]{1,0:T(8,128)}, u32[]{:S(2)}) copy-start(f32[16,768]{1,0:T(8,128)} %copy-done.72) | copy-start | bytes 147460
  663.6 85.0 %copy-start.84 = (bf16[16,768]{1,0:T(8,128)(2,1)S(1)}, bf16[16,768]{1,0:T(8,128)(2,1)}, u32[]{:S(2)}) copy-start(bf16[16,768]{1,0:T(8,128)(2,1)} %param.47) | copy-start | bytes 73732
  663.6 85.0 %copy-start.127 = (f32[16]{0:T(128)S(1)}, f32[16]{0:T(128)}, u32[]{:S(2)}) copy-start(f32[16]{0:T(128)} %copy-done.126) | copy-start | bytes 196
  663.6 86.4 %copy-start.9 = (bf16[1024,768]{1,0:T(8,128)(2,1)S(1)}, bf16[1024,768]{1,0:T(8,128)(2,1)}, u32[]{:S(2)}) copy-start(bf16[1024,768]{1,0:T(8,128)(2,1)} %param.27) | copy-start | bytes 4718596
  663.7 86.4 %copy-start.87 = (f32[1024]{0:T(1024)S(1)}, f32[1024]{0:T(1024)}, u32[]{:S(2)}) copy-start(f32[1024]{0:T(1024)} %copy-done.86) | copy-start | bytes 12292
  664.3 88.6 %copy-start.101 = (f32[1024]{0:T(1024)S(1)}, f32[1024]{0:T(1024)}, u32[]{:S(2)}) copy-start(f32[1024]{0:T(1024)} %copy-done.100) | copy-start | bytes 12292
  664.3 88.6 %copy-start.95 = (f32[1024]{0:T(1024)S(1)}, f32[1024]{0:T(1024)}, u32[]{:S(2)}) copy-start(f32[1024]{0:T(1024)} %copy-done.94) | copy-start | bytes 12292
  (145 other events, 639.3 us)
Sparse Core Ops, SparseCore 0:
  14.3 14.8 all-gather.4
  258.7 8.6 reduce-scatter.8
  269.0 13.2 all-gather.8
  285.0 8.5 reduce-scatter.10
  295.7 13.2 all-gather.6
  377.3 12.0 reduce-scatter.16
  391.7 12.0 reduce-scatter.12
  406.6 8.5 reduce-scatter.18
  418.1 8.5 reduce-scatter.14
  428.7 13.2 all-gather.10
  626.5 6.5 reduce-scatter.22
  635.8 12.0 reduce-scatter.20
  663.7 400.6 all-reduce.6
where the time goes:
time: 1090 us; the launch traced here: 1080 us
  waiting for transfers between devices  359 us (33%)
  matrix products  224 us (21%)
  blocking collectives  207 us (19%)
  local copies, waits for them, and re-layouts  186 us (17%)
  other arithmetic  62.2 us (6%)
  between operations  16.1 us (1%)
  starting transfers between devices  14.9 us (1%)
  loops' own time  14.4 us (1%)
    psum x1, waiting for transfers between devices, per_device(): lax.psum((w_query_grad, b_query_grad, w_key_grad, w_value_grad, b_value_g...  264 us
    psum x1, blocking collectives, per_device(): lax.psum((w_query_grad, b_query_grad, w_key_grad, w_value_grad, b_value_g...  78.8 us
    psum x1, blocking collectives, per_device(): glob_total = lax.psum(glob_part_tot, 'seq')  78.5 us
    dot_general x6, matrix products, mat_prod(): return jnp.dot(left, right, preferred_element_type=jnp.float32)  53.8 us
    unnamed x289, local copies, waits for them, and re-layouts  48.3 us
    psum x1, blocking collectives, per_device(): lax.psum((gain_attn_tok + gain_attn_glob, shift_attn_tok + shift_attn_glo...  41.3 us
    dot_general x26, matrix products, scores_of(): jnp.einsum('rhe,khe->hrk', queries, key_rows, preferred_element_type=jnp....  40.6 us
    all_gather x4, waiting for transfers between devices, pair_gather(): lax.all_gather(tok_part, 'tp', axis=0, tiled=True)  39.2 us
  transfers between devices with their start and end apart: 25, of which 17 were waited for; matrix products, arithmetic and copies ran while one was open for 15% of the time, Pallas kernels for 0%

commit v1 on v0

v1 whole, which is shorter than its diff:
```python
import functools

import jax
import jax.numpy as jnp
from jax import lax
from jax.experimental import pallas as pl
from jax.experimental.pallas import tpu as pltpu
from jax.sharding import PartitionSpec as P

HD = 64
BLOCK = 512
GLOB = 128
GROUP_BLOCKS = 32
EPS = 1e-05
SCALE = 0.125
NEG = -1e30
TILE = 256
PAIR = 2 * HD
LANES = 128
STATS = 16
F32 = jnp.float32
BF16 = jnp.bfloat16
VMEM_BYTES = 56 * 2**20


def nn(left, right):
    return jnp.dot(left, right, preferred_element_type=F32)


def nt(left, right):
    return lax.dot_general(left, right, (((1,), (1,)), ((), ())), preferred_element_type=F32)


def tn(left, right):
    return lax.dot_general(left, right, (((0,), (0,)), ((), ())), preferred_element_type=F32)


def normed(values):
    row_mean = jnp.mean(values, axis=-1, keepdims=True)
    centred = values - row_mean
    row_var = jnp.mean(centred * centred, axis=-1, keepdims=True)
    inv = lax.rsqrt(row_var + EPS)
    return centred * inv, inv


def norm_back(xhat, inv, gain_vec, cotangent):
    scaled = cotangent * gain_vec
    mean_one = jnp.mean(scaled, axis=-1, keepdims=True)
    mean_two = jnp.mean(scaled * xhat, axis=-1, keepdims=True)
    return inv * (scaled - mean_one - xhat * mean_two)


def full(shape):
    zeros = (0,) * len(shape)
    return pl.BlockSpec(shape, lambda *_: zeros, pipeline_mode=pl.Buffered(1))


def params(dims=1):
    return pltpu.CompilerParams(
        vmem_limit_bytes=VMEM_BYTES, dimension_semantics=("arbitrary",) * dims
    )


def cost(flops, nbytes, trans=0):
    return pl.CostEstimate(flops=int(flops), bytes_accessed=int(nbytes), transcendentals=int(trans))


def head_lanes(head):
    lane = lax.broadcasted_iota(jnp.int32, (1, LANES), 1)
    here = jnp.where(lane < HD, 1.0, 0.0)
    mine = here if head == 0 else 1.0 - here
    return mine.astype(BF16), (1.0 - mine).astype(BF16)


def lane_one(slot):
    lane = lax.broadcasted_iota(jnp.int32, (1, LANES), 1)
    return jnp.where((lane == slot) | (lane == slot + HD), 1.0, 0.0).astype(BF16)


def project_body(x_ref, gain_ref, shift_ref, own_ref, par_ref, bias_ref, scale_ref, *rest):
    qkv_ref, turned_ref = rest[-2:]
    xhat, _ = normed(x_ref[...].astype(F32))
    hidden = (xhat * gain_ref[...] + shift_ref[...]).astype(BF16)
    turned_ref[...] = hidden.T
    width = own_ref.shape[1]
    for half, weight in enumerate((own_ref, par_ref)):
        cols = slice(half * width, (half + 1) * width)
        made = nn(hidden, weight[...])
        qkv_ref[:, cols] = ((made + bias_ref[:, cols]) * scale_ref[:, cols]).astype(BF16)


def project(x, gain, shift, w_own, w_par, bias, scale, rows_all, first, held=None):
    rows, dim = x.shape
    width = 2 * w_own.shape[1]
    tiles = rows // TILE
    vec = full((1, dim))
    specs = [
        pl.BlockSpec((TILE, dim), lambda i: (i, 0)),
        vec,
        vec,
        full(w_own.shape),
        full(w_par.shape),
        full((1, width)),
        full((1, width)),
    ]
    operands = [x, gain, shift, w_own, w_par, bias, scale]
    aliases = {}
    if held is not None:
        aliases = {len(operands): 0, len(operands) + 1: 1}
        operands += list(held)
        specs += [pl.BlockSpec(memory_space=pl.ANY)] * 2
    return pl.pallas_call(
        project_body,
        grid=(tiles,),
        in_specs=specs,
        out_specs=[
            pl.BlockSpec((TILE, width), lambda i: (i + first, 0)),
            pl.BlockSpec((dim, TILE), lambda i: (0, i + first)),
        ],
        out_shape=[
            jax.ShapeDtypeStruct((rows_all, width), BF16),
            jax.ShapeDtypeStruct((dim, rows_all), BF16),
        ],
        input_output_aliases=aliases,
        compiler_params=params(),
        cost_estimate=cost(2 * rows * dim * width, 2 * (rows * (2 * dim + width) + dim * width)),
        name="project",
    )(*operands)


def pair_column(kind, pairs):
    half = pairs // 2
    return lambda p: (p // half) * 3 * half + kind * half + p % half


def glob_forward_body(q_ref, k_ref, v_ref, augk_ref, augq_ref, out_ref):
    rows_all = k_ref.shape[0]
    count = augq_ref.shape[0]
    queries = q_ref[rows_all - count :, :]
    keys = k_ref[...]
    values_turned = v_ref[...].T
    for head in range(2):
        mine, other = head_lanes(head)
        key_head = keys * mine + augk_ref[...] * other
        query_head = queries * mine + augq_ref[...] * other
        scores = nt(key_head, query_head)
        top = jnp.max(scores, axis=0, keepdims=True)
        weights = jnp.exp(scores - top)
        total = jnp.sum(weights, axis=0, keepdims=True)
        summed = nn(values_turned[head * HD : (head + 1) * HD, :], weights.astype(BF16))
        out_ref[head, :HD, :] = (summed / total).astype(BF16)
        write_stats(out_ref, head, top + jnp.log(total))


def write_stats(out_ref, head, lse):
    first = lse.astype(BF16).astype(F32)
    second = (lse - first).astype(BF16).astype(F32)
    third = lse - first - second
    row = lax.broadcasted_iota(jnp.int32, (STATS, lse.shape[1]), 0)
    held = jnp.where(row == 0, first, jnp.where(row == 1, second, jnp.where(row == 2, third, 0.0)))
    out_ref[head, HD : HD + STATS, :] = held.astype(BF16)


def glob_forward(qkv, augk, augq, pairs):
    rows_all = qkv.shape[0]
    count = augq.shape[0]

    def block(kind):
        column = pair_column(kind, pairs)
        return pl.BlockSpec((rows_all, LANES), lambda p: (0, column(p)))

    work = 2 * pairs * rows_all * count
    return pl.pallas_call(
        glob_forward_body,
        grid=(pairs,),
        in_specs=[block(0), block(1), block(2), full(augk.shape), full(augq.shape)],
        out_specs=pl.BlockSpec((2, HD + STATS, count), lambda p: (p, 0, 0)),
        out_shape=jax.ShapeDtypeStruct((2 * pairs, HD + STATS, count), BF16),
        compiler_params=params(),
        cost_estimate=cost(work * 2 * 512, qkv.size * 2, work),
        name="glob_forward",
    )(qkv, qkv, qkv, augk, augq)


def read_stats(ref, head):
    held = ref[head, HD : HD + STATS, :].astype(F32)
    return held[0:1] + held[1:2] + held[2:3]


def merge_head(left_ref, right_ref, head):
    lse_left, lse_right = read_stats(left_ref, head), read_stats(right_ref, head)
    top = jnp.maximum(lse_left, lse_right)
    weight_left, weight_right = jnp.exp(lse_left - top), jnp.exp(lse_right - top)
    total = weight_left + weight_right
    out_left = left_ref[head, :HD, :].astype(F32)
    out_right = right_ref[head, :HD, :].astype(F32)
    merged = (out_left * weight_left + out_right * weight_right) / total
    return merged, top + jnp.log(total)


def merge_body(left_ref, right_ref, out_ref):
    for head in range(left_ref.shape[0]):
        merged, lse = merge_head(left_ref, right_ref, head)
        out_ref[head, :HD, :] = merged.astype(BF16)
        write_stats(out_ref, head, lse)


def merge(left, right):
    return pl.pallas_call(
        merge_body,
        out_shape=jax.ShapeDtypeStruct(left.shape, BF16),
        compiler_params=pltpu.CompilerParams(vmem_limit_bytes=VMEM_BYTES),
        cost_estimate=cost(left.size * 8, left.size * 6),
        name="merge",
    )(left, right)


def local_forward_body(
    docs_ref, q_ref, k_ref, v_ref, kg_ref, vg_ref, augk_ref, high_ref, low_ref, turned_ref, lse_ref
):
    keys = jnp.concatenate([k_ref[...], kg_ref[...]], 0)
    values_turned = jnp.concatenate([v_ref[...], vg_ref[...]], 0).T
    bias = jnp.concatenate([augk_ref[...], jnp.zeros((GLOB, LANES), BF16)], 0)
    outs = []
    for head in range(2):
        mine, other = head_lanes(head)
        key_head = keys * mine + bias * other
        query_head = q_ref[...] * mine + lane_one(0) * other
        scores = nt(key_head, query_head)
        top = jnp.max(scores, axis=0, keepdims=True)
        weights = jnp.exp(scores - top)
        total = jnp.sum(weights, axis=0, keepdims=True)
        summed = nn(values_turned[head * HD : (head + 1) * HD, :], weights.astype(BF16))
        outs.append(summed / total)
        lse_ref[0, 0, head : head + 1, :] = top + jnp.log(total)
    turned = jnp.concatenate(outs, 0)
    turned_ref[...] = turned.astype(BF16)
    straight = turned.T
    high = straight.astype(BF16)
    high_ref[...] = high
    low_ref[...] = (straight - high.astype(F32)).astype(BF16)


def local_forward(docs, qkv, augk, pairs, blocks):
    rows_all = qkv.shape[0]
    local_rows = blocks * BLOCK
    glob_first = local_rows // GLOB

    def block(kind):
        column = pair_column(kind, pairs)
        return pl.BlockSpec((BLOCK, LANES), lambda b, p, docs: (b, column(p)))

    def glob_block(kind):
        column = pair_column(kind, pairs)
        return pl.BlockSpec((GLOB, LANES), lambda b, p, docs: (glob_first + docs[b], column(p)))

    work = 2 * pairs * local_rows * (BLOCK + GLOB)
    width = pairs * LANES
    straight = pl.BlockSpec((BLOCK, LANES), lambda b, p, docs: (b, p))
    return pl.pallas_call(
        local_forward_body,
        grid_spec=pltpu.PrefetchScalarGridSpec(
            num_scalar_prefetch=1,
            grid=(blocks, pairs),
            in_specs=[
                block(0),
                block(1),
                block(2),
                glob_block(1),
                glob_block(2),
                pl.BlockSpec((BLOCK, LANES), lambda b, p, docs: (b, 0)),
            ],
            out_specs=[
                straight,
                straight,
                pl.BlockSpec((LANES, BLOCK), lambda b, p, docs: (p, b)),
                pl.BlockSpec((1, 1, 2, BLOCK), lambda b, p, docs: (b, p, 0, 0)),
            ],
        ),
        out_shape=[
            jax.ShapeDtypeStruct((rows_all, width), BF16),
            jax.ShapeDtypeStruct((rows_all, width), BF16),
            jax.ShapeDtypeStruct((width, rows_all), BF16),
            jax.ShapeDtypeStruct((blocks, pairs, 2, BLOCK), F32),
        ],
        compiler_params=params(2),
        cost_estimate=cost(work * 2 * 512, qkv.size * 2, work),
        name="local_forward",
    )(docs, qkv, qkv, qkv, qkv, qkv, augk)


def middle_of(out_high, x, own_ref, par_ref, bias_ref, gain_ref, shift_ref):
    half = own_ref.shape[0]
    branch = nn(out_high[:, :half], own_ref[...]) + nn(out_high[:, half:], par_ref[...])
    middle = x.astype(F32) + branch + bias_ref[...]
    xhat, _ = normed(middle)
    hidden = (xhat * gain_ref[...] + shift_ref[...]).astype(BF16)
    return middle, hidden


def middle_body(
    out_ref, x_ref, own_ref, par_ref, bias_ref, gain_ref, shift_ref, mid_ref, hid_ref, turned_ref
):
    middle, hidden = middle_of(
        out_ref[...], x_ref[...], own_ref, par_ref, bias_ref, gain_ref, shift_ref
    )
    mid_ref[...] = middle
    hid_ref[...] = hidden
    turned_ref[...] = hidden.T


def middle_local(out_high, x, w_own, w_par, bias, gain, shift):
    rows_all, dim = out_high.shape
    rows = x.shape[0]
    row = pl.BlockSpec((TILE, dim), lambda i: (i, 0))
    vec = full((1, dim))
    return pl.pallas_call(
        middle_body,
        grid=(rows // TILE,),
        in_specs=[row, row, full(w_own.shape), full(w_par.shape), vec, vec, vec],
        out_specs=[row, row, pl.BlockSpec((dim, TILE), lambda i: (0, i))],
        out_shape=[
            jax.ShapeDtypeStruct((rows_all, dim), F32),
            jax.ShapeDtypeStruct((rows_all, dim), BF16),
            jax.ShapeDtypeStruct((dim, rows_all), BF16),
        ],
        compiler_params=params(),
        cost_estimate=cost(2 * rows * dim * dim, 12 * rows * dim + 2 * dim * dim),
        name="middle_local",
    )(out_high, x, w_own, w_par, bias, gain, shift)


def middle_glob_body(own_out_ref, par_out_ref, x_ref, own_ref, par_ref, bias_ref, gain_ref, shift_ref, *rest):
    mid_ref, hid_ref, turned_ref, high_ref, low_ref, out_turned_ref, lse_ref = rest[-7:]
    heads = own_out_ref.shape[0]
    parts = [own_out_ref[head, :HD, :] for head in range(heads)]
    parts += [par_out_ref[head, :HD, :] for head in range(heads)]
    turned = jnp.concatenate(parts, 0)
    out_turned_ref[...] = turned
    high = turned.T
    high_ref[...] = high
    low_ref[...] = jnp.zeros_like(high)
    stats = [read_stats(own_out_ref, head) for head in range(heads)]
    stats += [read_stats(par_out_ref, head) for head in range(heads)]
    spare = lse_ref.shape[0] - 2 * heads
    lse_ref[...] = jnp.concatenate(stats + [jnp.zeros((spare, x_ref.shape[0]), F32)], 0)
    middle, hidden = middle_of(high, x_ref[...], own_ref, par_ref, bias_ref, gain_ref, shift_ref)
    mid_ref[...] = middle
    hid_ref[...] = hidden
    turned_ref[...] = hidden.T


def middle_glob(own_out, par_out, x, w_own, w_par, bias, gain, shift, held):
    rows, dim = x.shape
    rows_all = held[0].shape[0]
    first = rows_all // rows - 1
    vec = full((1, dim))
    row = pl.BlockSpec((rows, dim), lambda i: (first, 0))
    col = pl.BlockSpec((dim, rows), lambda i: (0, first))
    lse_rows = 16
    return pl.pallas_call(
        middle_glob_body,
        grid=(1,),
        in_specs=[
            full(own_out.shape),
            full(par_out.shape),
            full((rows, dim)),
            full(w_own.shape),
            full(w_par.shape),
            vec,
            vec,
            vec,
        ]
        + [pl.BlockSpec(memory_space=pl.ANY)] * 6,
        out_specs=[row, row, col, row, row, col, full((lse_rows, rows))],
        out_shape=[jax.ShapeDtypeStruct(h.shape, h.dtype) for h in held]
        + [jax.ShapeDtypeStruct((lse_rows, rows), F32)],
        input_output_aliases={8 + i: i for i in range(6)},
        compiler_params=params(),
        cost_estimate=cost(2 * rows * dim * dim, 12 * rows * dim + 2 * dim * dim),
        name="middle_glob",
    )(own_out, par_out, x, w_own, w_par, bias, gain, shift, *held)


def ffn_body(
    hid_ref, turned_ref, dz_ref, up_ref, bias_ref, down_ref, mask_ref,
    dnorm_ref, out_ref, grads_ref, bias_grad_ref, act_s, dup_s,
):
    step = pl.program_id(0)
    rows_all, dim = hid_ref.shape
    chunk = up_ref.shape[1]
    tiles = rows_all // TILE
    bias_grad = jnp.zeros((1, chunk), F32)
    for tile in range(tiles):
        rows = slice(tile * TILE, (tile + 1) * TILE)
        up = nn(hid_ref[rows, :], up_ref[...]) + bias_ref[...]
        share = 0.5 * (1.0 + lax.erf(up * (2.0**-0.5)))
        density = jnp.exp(up * up * -0.5) * 0.3989422804014327
        active = (up * share).astype(BF16)
        slope = share + up * density
        d_up = (nt(dz_ref[rows, :], down_ref[...]) * slope).astype(BF16)
        d_norm = nt(d_up, up_ref[...])
        out = nn(active, down_ref[...])

        @pl.when(step == 0)
        def _():
            dnorm_ref[rows, :] = d_norm
            out_ref[rows, :] = out

        @pl.when(step > 0)
        def _():
            dnorm_ref[rows, :] += d_norm
            out_ref[rows, :] += out

        if tile == tiles - 1:
            mask = mask_ref[...]
            d_up = (d_up.astype(F32) * mask).astype(BF16)
            active = (active.astype(F32) * mask).astype(BF16)
        bias_grad += jnp.sum(d_up.astype(F32), axis=0, keepdims=True)
        act_s[rows, :] = active
        dup_s[rows, :] = d_up
    bias_grad_ref[...] = bias_grad
    up_grad = nn(turned_ref[...], dup_s[...]).astype(BF16)
    down_grad = tn(act_s[...], dz_ref[...]).astype(BF16)
    place = 0
    for grad in (up_grad, down_grad):
        rows = grad.shape[0]
        for col in range(grad.shape[1] // LANES):
            grads_ref[0, place : place + rows, :] = grad[:, col * LANES : (col + 1) * LANES]
            place += rows


def ffn_half(hidden, turned, dz, w_up, b_up, w_down, mask):
    rows_all, dim = hidden.shape
    units = w_up.shape[1]
    chunk = TILE
    steps = units // chunk
    packed = 2 * chunk * dim // LANES
    return pl.pallas_call(
        ffn_body,
        grid=(steps,),
        in_specs=[
            full(hidden.shape),
            full(turned.shape),
            full(dz.shape),
            pl.BlockSpec((dim, chunk), lambda j: (0, j)),
            pl.BlockSpec((1, chunk), lambda j: (0, j)),
            pl.BlockSpec((chunk, dim), lambda j: (j, 0)),
            full(mask.shape),
        ],
        out_specs=[
            full((rows_all, dim)),
            full((rows_all, dim)),
            pl.BlockSpec((1, packed, LANES), lambda j: (j, 0, 0)),
            pl.BlockSpec((1, chunk), lambda j: (0, j)),
        ],
        out_shape=[
            jax.ShapeDtypeStruct((rows_all, dim), F32),
            jax.ShapeDtypeStruct((rows_all, dim), F32),
            jax.ShapeDtypeStruct((steps, packed, LANES), BF16),
            jax.ShapeDtypeStruct((1, units), F32),
        ],
        scratch_shapes=[pltpu.VMEM((rows_all, chunk), BF16), pltpu.VMEM((rows_all, chunk), BF16)],
        compiler_params=params(),
        cost_estimate=cost(
            12 * rows_all * dim * units, rows_all * dim * 14 + units * dim * 8, 2 * rows_all * units
        ),
        name="ffn_half",
    )(hidden, turned, dz, w_up, b_up, w_down, mask)


def middle_back_body(
    dn_one_ref, dn_two_ref, mid_ref, dz_ref, high_ref, low_ref, out_turned_ref, own_ref, par_ref,
    gain_ref, mask_ref, dmid_ref, dattn_ref, delta_ref, grads_ref, sums_ref, acc_s,
):
    step = pl.program_id(0)
    dim = mid_ref.shape[1]
    half = own_ref.shape[0]
    xhat, inv = normed(mid_ref[...])
    dn = dn_one_ref[...] + dn_two_ref[...]
    dz = dz_ref[...].astype(F32)
    d_mid = dz + norm_back(xhat, inv, gain_ref[...], dn)
    dmid_ref[...] = d_mid
    d_branch = d_mid.astype(BF16)
    for part, weight in enumerate((own_ref, par_ref)):
        dattn_ref[:, part * half : (part + 1) * half] = nt(d_branch, weight[...]).astype(BF16)
    straight = high_ref[...].astype(F32) + low_ref[...].astype(F32)
    product = dattn_ref[...].astype(F32) * straight
    first = product.astype(BF16)
    second = (product - first.astype(F32)).astype(BF16)
    head = lax.broadcasted_iota(jnp.int32, (delta_ref.shape[0], dim), 0)
    column = lax.broadcasted_iota(jnp.int32, (delta_ref.shape[0], dim), 1)
    picked = jnp.where((column >= head * HD) & (column < (head + 1) * HD), 1.0, 0.0).astype(BF16)
    delta_ref[...] = nt(picked, first) + nt(picked, second)
    mask = mask_ref[...]
    masked = (d_branch.astype(F32) * mask).astype(BF16)
    made = nn(out_turned_ref[...], masked)
    sums = [
        jnp.sum(dn * xhat * mask, axis=0, keepdims=True),
        jnp.sum(dn * mask, axis=0, keepdims=True),
        jnp.sum(masked.astype(F32), axis=0, keepdims=True),
        jnp.sum(dz * mask, axis=0, keepdims=True),
    ]
    sums = jnp.concatenate(sums + [jnp.zeros((4, dim), F32)], 0)

    @pl.when(step == 0)
    def _():
        acc_s[...] = made
        sums_ref[...] = sums

    @pl.when(step > 0)
    def _():
        acc_s[...] += made
        sums_ref[...] += sums

    @pl.when(step == pl.num_programs(0) - 1)
    def _():
        for part in range(2):
            for col in range(dim // LANES):
                grads_ref[part, col * half : (col + 1) * half, :] = acc_s[
                    part * half : (part + 1) * half, col * LANES : (col + 1) * LANES
                ].astype(BF16)


def middle_back(dn_one, dn_two, middle, dz, high, low, out_turned, w_own, w_par, gain, mask):
    rows_all, dim = middle.shape
    row = pl.BlockSpec((TILE, dim), lambda i: (i, 0))
    col = pl.BlockSpec((dim, TILE), lambda i: (0, i))
    lse_rows = 16
    packed = w_own.size // LANES
    return pl.pallas_call(
        middle_back_body,
        grid=(rows_all // TILE,),
        in_specs=[
            row, row, row, row, row, row, col, full(w_own.shape), full(w_par.shape),
            full((1, dim)), pl.BlockSpec((TILE, 1), lambda i: (i, 0)),
        ],
        out_specs=[
            row,
            row,
            pl.BlockSpec((lse_rows, TILE), lambda i: (0, i)),
            full((2, packed, LANES)),
            full((8, dim)),
        ],
        out_shape=[
            jax.ShapeDtypeStruct((rows_all, dim), F32),
            jax.ShapeDtypeStruct((rows_all, dim), BF16),
            jax.ShapeDtypeStruct((lse_rows, rows_all), F32),
            jax.ShapeDtypeStruct((2, packed, LANES), BF16),
            jax.ShapeDtypeStruct((8, dim), F32),
        ],
        scratch_shapes=[pltpu.VMEM((dim, dim), F32)],
        compiler_params=params(),
        cost_estimate=cost(4 * rows_all * dim * dim, rows_all * dim * 28),
        name="middle_back",
    )(dn_one, dn_two, middle, dz, high, low, out_turned, w_own, w_par, gain, mask)


def attention_back_body(
    docs_ref, q_ref, k_ref, v_ref, do_ref, lse_ref, lseg_ref, delta_ref, augk_ref, augq_ref,
    dq_ref, dk_ref, dv_ref, key_s, value_s, turned_s, dk_s, dv_s,
):
    pair = pl.program_id(0)
    rows_all = q_ref.shape[0]
    count = augq_ref.shape[0]
    local_rows = rows_all - count
    blocks = local_rows // BLOCK
    turned_s[...] = k_ref[...].T
    dk_s[...] = jnp.zeros_like(dk_s)
    dv_s[...] = jnp.zeros_like(dv_s)
    dq_parts = [[] for _ in range(blocks + 1)]
    for head in range(2):
        mine, other = head_lanes(head)
        key_s[...] = k_ref[...] * mine + augk_ref[...] * other
        value_s[...] = v_ref[...] * mine
        head_rows = slice(head * HD, (head + 1) * HD)
        index = 2 * pair + head

        def grads(key_cat, value_cat, turned_cat, query_rows, aug, lse):
            queries = q_ref[query_rows, :] * mine
            douts = do_ref[query_rows, :] * mine
            delta = delta_ref[pl.ds(index, 1), query_rows]
            probs = jnp.exp(nt(key_cat, queries + aug * other) - lse)
            d_scores = (probs * (nt(value_cat, douts) - delta)).astype(BF16)
            d_key = nn(d_scores, queries)
            d_value = nn(probs.astype(BF16), douts)
            return nn(turned_cat, d_scores), d_key, d_value

        for block in range(blocks):
            rows = slice(block * BLOCK, (block + 1) * BLOCK)
            start = pl.multiple_of(local_rows + docs_ref[block] * GLOB, GLOB)
            doc_rows = pl.ds(start, GLOB)
            key_cat = jnp.concatenate([key_s[rows, :], key_s[doc_rows, :]], 0)
            value_cat = jnp.concatenate([value_s[rows, :], value_s[doc_rows, :]], 0)
            turned_cat = jnp.concatenate(
                [turned_s[head_rows, rows], turned_s[head_rows, doc_rows]], 1
            )
            d_query, d_key, d_value = grads(
                key_cat, value_cat, turned_cat, rows, lane_one(0), lse_ref[block, 0, head : head + 1, :]
            )
            dq_parts[block].append(d_query)
            dk_s[rows, :] += d_key[:BLOCK]
            dk_s[doc_rows, :] += d_key[BLOCK:]
            dv_s[rows, :] += d_value[:BLOCK]
            dv_s[doc_rows, :] += d_value[BLOCK:]
        rows = slice(local_rows, rows_all)
        d_query, d_key, d_value = grads(
            key_s[...], value_s[...], turned_s[head_rows, :], rows, augq_ref[...],
            lseg_ref[pl.ds(index, 1), :],
        )
        dq_parts[blocks].append(d_query)
        dk_s[...] += d_key
        dv_s[...] += d_value
    for block in range(blocks + 1):
        first = block * BLOCK
        made = jnp.concatenate(dq_parts[block], 0).T
        dq_ref[first : first + made.shape[0], :] = (made.astype(BF16).astype(F32) * SCALE).astype(BF16)
    dk_ref[...] = dk_s[...].astype(BF16)
    dv_ref[...] = dv_s[...].astype(BF16)


def attention_back(docs, qkv, d_attn, lse, lse_glob, delta, augk, augq, pairs):
    rows_all = qkv.shape[0]
    count = augq.shape[0]
    blocks = (rows_all - count) // BLOCK

    def block(kind):
        column = pair_column(kind, pairs)
        return pl.BlockSpec((rows_all, LANES), lambda p, docs: (0, column(p)))

    straight = pl.BlockSpec((rows_all, LANES), lambda p, docs: (0, p))
    shape = jax.ShapeDtypeStruct((rows_all, pairs * LANES), BF16)
    work = 2 * pairs * (blocks * BLOCK * (BLOCK + GLOB) + rows_all * count)
    return pl.pallas_call(
        attention_back_body,
        grid_spec=pltpu.PrefetchScalarGridSpec(
            num_scalar_prefetch=1,
            grid=(pairs,),
            in_specs=[
                block(0),
                block(1),
                block(2),
                straight,
                pl.BlockSpec((blocks, 1, 2, BLOCK), lambda p, docs: (0, p, 0, 0)),
                full(lse_glob.shape),
                full(delta.shape),
                full(augk.shape),
                full(augq.shape),
            ],
            out_specs=[straight] * 3,
            scratch_shapes=[
                pltpu.VMEM((rows_all, LANES), BF16),
                pltpu.VMEM((rows_all, LANES), BF16),
                pltpu.VMEM((LANES, rows_all), BF16),
                pltpu.VMEM((rows_all, LANES), F32),
                pltpu.VMEM((rows_all, LANES), F32),
            ],
        ),
        out_shape=[shape] * 3,
        compiler_params=params(),
        cost_estimate=cost(work * 5 * 512, qkv.size * 4, work),
        name="attention_back",
    )(docs, qkv, qkv, qkv, d_attn, lse, lse_glob, delta, augk, augq)


def project_grad_body(turned_ref, dq_ref, dk_ref, dv_ref, grads_ref, sums_ref):
    step = pl.program_id(0)
    width = dq_ref.shape[1]
    for kind, ref in enumerate((dq_ref, dk_ref, dv_ref)):
        made = nn(turned_ref[...], ref[...]).astype(BF16)
        for col in range(width // LANES):
            grads_ref[kind * (width // LANES) + col, :, :] = made[:, col * LANES : (col + 1) * LANES]

    @pl.when(step == 0)
    def _():
        sums_ref[...] = jnp.zeros_like(sums_ref)
        for slot, ref in enumerate((dq_ref, dv_ref)):
            sums_ref[slot : slot + 1, :] = jnp.sum(ref[...].astype(F32), axis=0, keepdims=True)


def project_grad(turned, dq, dk, dv, half):
    dim, rows_all = turned.shape
    width = dq.shape[1] // 2
    grads = pl.BlockSpec((rows_all, width), lambda i: (0, half), pipeline_mode=pl.Buffered(1))
    blocks = 3 * width // LANES
    return pl.pallas_call(
        project_grad_body,
        grid=(dim // TILE,),
        in_specs=[pl.BlockSpec((TILE, rows_all), lambda i: (i, 0)), grads, grads, grads],
        out_specs=[pl.BlockSpec((blocks, TILE, LANES), lambda i: (0, i, 0)), full((8, width))],
        out_shape=[
            jax.ShapeDtypeStruct((blocks, dim, LANES), BF16),
            jax.ShapeDtypeStruct((8, width), F32),
        ],
        compiler_params=params(),
        cost_estimate=cost(6 * rows_all * dim * width, rows_all * (dim + 3 * width) * 2),
        name="project_grad",
    )(turned, dq, dk, dv)


def input_back_body(
    dq_ref, dk_ref, dv_ref, own_ref, par_ref, x_ref, xg_ref, dmid_ref, gain_ref,
    tokens_ref, glob_ref, sums_ref,
):
    step = pl.program_id(0)
    last = pl.num_programs(0) - 1
    half = own_ref.shape[1] // 3
    d_hidden = None
    for part, weight in enumerate((own_ref, par_ref)):
        cols = slice(part * half, (part + 1) * half)
        joined = jnp.concatenate([dq_ref[:, cols], dk_ref[:, cols], dv_ref[:, cols]], 1)
        made = nt(joined, weight[...])
        d_hidden = made if d_hidden is None else d_hidden + made

    @pl.when(step == 0)
    def _():
        sums_ref[...] = jnp.zeros_like(sums_ref)

    def add_sums(xhat):
        sums_ref[0:1, :] += jnp.sum(d_hidden * xhat, axis=0, keepdims=True)
        sums_ref[1:2, :] += jnp.sum(d_hidden, axis=0, keepdims=True)

    @pl.when(step < last)
    def _():
        xhat, inv = normed(x_ref[...].astype(F32))
        tokens_ref[...] = dmid_ref[...] + norm_back(xhat, inv, gain_ref[...], d_hidden)
        add_sums(xhat)

    @pl.when(step == last)
    def _():
        xhat, _ = normed(xg_ref[...].astype(F32))
        glob_ref[...] = d_hidden.astype(BF16)
        add_sums(xhat)


def input_back(dq, dk, dv, w_own, w_par, x, x_glob, d_mid, gain):
    rows_all, dim = dq.shape
    tiles = rows_all // TILE
    row = pl.BlockSpec((TILE, dim), lambda i: (i, 0))
    local = pl.BlockSpec((TILE, dim), lambda i: (jnp.minimum(i, tiles - 2), 0))
    return pl.pallas_call(
        input_back_body,
        grid=(tiles,),
        in_specs=[
            row, row, row, full(w_own.shape), full(w_par.shape), local, full(x_glob.shape), row,
            full((1, dim)),
        ],
        out_specs=[local, full(x_glob.shape), full((8, dim))],
        out_shape=[
            jax.ShapeDtypeStruct(x.shape, F32),
            jax.ShapeDtypeStruct(x_glob.shape, BF16),
            jax.ShapeDtypeStruct((8, dim), F32),
        ],
        compiler_params=params(),
        cost_estimate=cost(6 * rows_all * dim * dim, rows_all * dim * 16 + 6 * dim * dim),
        name="input_back",
    )(dq, dk, dv, w_own, w_par, x, x_glob, d_mid, gain)


def glob_input_body(own_ref, par_ref, x_ref, dmid_ref, gain_ref, out_ref):
    d_hidden = own_ref[...].astype(F32) + par_ref[...].astype(F32)
    xhat, inv = normed(x_ref[...].astype(F32))
    out_ref[...] = dmid_ref[...] + norm_back(xhat, inv, gain_ref[...], d_hidden)


def glob_input(kept, received, x, d_mid, gain):
    return pl.pallas_call(
        glob_input_body,
        out_shape=jax.ShapeDtypeStruct(x.shape, F32),
        name="glob_input",
    )(kept, received, x, d_mid, gain)


def block_layout(doc_blocks, doc_tail, first_block, block_count, block_len):
    doc_ends = jnp.cumsum(doc_blocks)
    block_ids = first_block + jnp.arange(block_count, dtype=jnp.int32)
    doc_of = jnp.sum((block_ids[:, None] >= doc_ends[None, :]).astype(jnp.int32), axis=1)
    picked = doc_of[:, None] == jnp.arange(doc_ends.shape[0], dtype=jnp.int32)[None, :]
    last_end = jnp.sum(jnp.where(picked, doc_ends[None, :], 0), axis=1)
    tail_len = jnp.sum(jnp.where(picked, doc_tail[None, :], 0), axis=1)
    tail_all = jnp.where(block_ids == last_end - 1, tail_len, block_len)
    key_valid = jnp.arange(block_len, dtype=jnp.int32)[None, :] < tail_all[:, None]
    return (doc_of, key_valid)


def per_device(
    tokens, glob_tokens, w_query, b_query, w_key, w_value, b_value, w_out, b_out, w_up, b_up,
    w_down, b_down, gain_attn, shift_attn, gain_ffn, shift_ffn, doc_blocks, doc_tail,
    grad_tokens, grad_glob,
):
    seq_size = lax.axis_size("seq")
    seq_pos = lax.axis_index("seq")
    tp_pos = lax.axis_index("tp")
    rows, dim = tokens.shape
    own_glob = glob_tokens.shape[0]
    half = w_query.shape[1]
    pairs = 2 * half // PAIR
    blocks = rows // BLOCK
    glob_rows = 2 * GLOB
    rows_all = rows + glob_rows
    group_size = GROUP_BLOCKS // (2 * blocks)
    group_bits = group_size.bit_length() - 1
    seq_bits = seq_size.bit_length() - 1
    group_pos = seq_pos % group_size
    own_first = (group_pos * 2 + tp_pos) * own_glob

    def flip(value, bit):
        return lax.ppermute(value, "seq", [(s, s ^ (1 << bit)) for s in range(seq_size)])

    def swap(value):
        return lax.ppermute(value, "tp", [(0, 1), (1, 0)])

    def row_vec(vector):
        return vector.reshape(1, -1)

    qkv_own = jnp.concatenate([w_query, w_key, w_value], 1)
    qkv_par = swap(qkv_own)
    out_par = swap(w_out)
    up_par = swap(w_up)
    down_par = swap(w_down)
    vec_own = jnp.concatenate([b_query, b_value, b_up])
    vec_par = swap(vec_own)

    gathered = jnp.stack([glob_tokens, grad_glob])[None]
    for bit in range(group_bits):
        upper = (group_pos >> bit) & 1 == 1
        other = flip(gathered, bit)
        gathered = jnp.where(
            upper,
            jnp.concatenate([other, gathered], 0),
            jnp.concatenate([gathered, other], 0),
        )
    other = swap(gathered)
    gathered = jnp.where(
        tp_pos == 1, jnp.stack([other, gathered], 1), jnp.stack([gathered, other], 1)
    )
    x_glob = gathered[:, :, 0].reshape(glob_rows, dim)
    dz_glob = gathered[:, :, 1].reshape(glob_rows, dim)
    dz_all = jnp.concatenate([grad_tokens, dz_glob], 0)

    first_block = (seq_pos * 2 + tp_pos) * blocks
    doc_of, key_valid = block_layout(doc_blocks, doc_tail, first_block, blocks, BLOCK)
    docs = doc_of - (seq_pos // group_size) * 2
    slot = jnp.arange(LANES, dtype=jnp.int32)[None, :] % HD
    valid = key_valid.reshape(-1)
    key_doc = jnp.concatenate(
        [jnp.repeat(docs, BLOCK), jnp.arange(glob_rows, dtype=jnp.int32) // GLOB]
    )
    is_glob = jnp.arange(rows_all) >= rows
    usable = jnp.concatenate([valid, jnp.ones((glob_rows,), bool)])
    closed = jnp.where(
        slot == 0,
        ~usable[:, None],
        jnp.where(
            slot == 3,
            is_glob[:, None],
            ((slot == 1) | (slot == 2)) & ~(usable & True)[:, None]
            | ((slot == 1) & (key_doc != 0)[:, None])
            | ((slot == 2) & (key_doc != 1)[:, None]),
        ),
    )
    augk = jnp.where(closed, NEG, 0.0).astype(BF16)
    glob_ids = jnp.arange(glob_rows, dtype=jnp.int32)
    owned = (glob_ids >= own_first) & (glob_ids < own_first + own_glob)
    augq = (
        ((slot == 1) & (glob_ids < GLOB)[:, None])
        | ((slot == 2) & (glob_ids >= GLOB)[:, None])
        | ((slot == 3) & ~owned[:, None])
    ).astype(BF16)
    mask_glob = owned.astype(F32)[:, None]
    mask_all = jnp.concatenate([jnp.ones((rows, 1), F32), mask_glob], 0)

    none = jnp.zeros((half,), F32)
    bias = row_vec(
        jnp.concatenate([b_query, none, b_value, vec_par[:half], none, vec_par[half : 2 * half]])
    )
    scale = row_vec(jnp.tile(jnp.repeat(jnp.array([SCALE, 1.0, 1.0], F32), half), 2))
    gain_a, shift_a, gain_f, shift_f = map(row_vec, (gain_attn, shift_attn, gain_ffn, shift_ffn))
    held = project(tokens, gain_a, shift_a, qkv_own, qkv_par, bias, scale, rows_all, 0)
    qkv, hidden_turned = project(
        x_glob, gain_a, shift_a, qkv_own, qkv_par, bias, scale, rows_all, rows // TILE, held
    )

    part = glob_forward(qkv, augk, augq, pairs)
    mine, theirs = part[:pairs], part[pairs:]
    state = merge(mine, swap(theirs))
    for bit in range(group_bits):
        state = merge(state, flip(state, bit))
    state_par = swap(state)
    high, low, out_turned, lse = local_forward(docs, qkv, augk, pairs, blocks)
    bias_out = row_vec(b_out)
    held = middle_local(high, tokens, w_out, out_par, bias_out, gain_f, shift_f)
    middle, hidden, ffn_turned, high, low, out_turned, lse_glob = middle_glob(
        state, state_par, x_glob, w_out, out_par, bias_out, gain_f, shift_f,
        [*held, high, low, out_turned],
    )

    b_up_par = row_vec(vec_par[2 * half :])
    dn_par, add_par, ffn_grad_par, up_sum_par = ffn_half(
        hidden, ffn_turned, dz_all, up_par, b_up_par, down_par, mask_glob
    )
    dn_own, add_own, ffn_grad_own, up_sum_own = ffn_half(
        hidden, ffn_turned, dz_all, w_up, row_vec(b_up), w_down, mask_glob
    )

    def add_pair(own, received):
        return (own.astype(F32) + received.astype(F32)).astype(BF16)

    def order_of(step):
        if seq_bits < 2:
            return step, step
        return step, (1, 0, *range(2, seq_bits))[step]

    def trade(value, step):
        zero, one = order_of(step)
        links = [(2 * s, 2 * (s ^ (1 << zero))) for s in range(seq_size)]
        links += [(2 * s + 1, 2 * (s ^ (1 << one)) + 1) for s in range(seq_size)]
        return lax.ppermute(value, ("seq", "tp"), links)

    def side_of(step):
        zero, one = order_of(step)
        return (seq_pos >> jnp.where(tp_pos == 0, zero, one)) & 1

    def reduce_all(value):
        for step in range(seq_bits):
            count = value.shape[0] // 2
            side = side_of(step)
            leaving = lax.dynamic_slice_in_dim(value, (1 - side) * count, count, 0)
            staying = lax.dynamic_slice_in_dim(value, side * count, count, 0)
            value = add_pair(staying, trade(leaving, step))
        for step in reversed(range(seq_bits)):
            side = side_of(step) == 1
            other = trade(value, step)
            value = jnp.where(
                side, jnp.concatenate([other, value], 0), jnp.concatenate([value, other], 0)
            )
        return value

    ffn_sum = reduce_all(
        add_pair(ffn_grad_own, swap(ffn_grad_par)).reshape(-1, LANES)
    )

    d_mid, d_attn, delta, out_grad, mid_sums = middle_back(
        dn_par, dn_own, middle, dz_all, high, low, out_turned, w_out, out_par, gain_f, mask_all
    )
    dq, dk, dv = attention_back(docs, qkv, d_attn, lse, lse_glob, delta, augk, augq, pairs)
    qkv_grad_par, qkv_sum_par = project_grad(hidden_turned, dq, dk, dv, 1)
    qkv_grad_own, qkv_sum_own = project_grad(hidden_turned, dq, dk, dv, 0)
    tokens_grad, d_hidden_glob, in_sums = input_back(
        dq, dk, dv, qkv_own, qkv_par, tokens, x_glob, d_mid, gain_a
    )

    rest = jnp.concatenate([mid_sums[:4], in_sums[:2]], 0).reshape(-1)

    def pack(qkv_grad, out_part, qkv_sum, up_sum):
        small = jnp.concatenate([rest, qkv_sum[0], qkv_sum[1], up_sum.reshape(-1)])
        small = small.reshape(-1, LANES).astype(BF16)
        whole = jnp.concatenate([qkv_grad.reshape(-1, LANES), out_part, small], 0)
        unit = 16 * seq_size
        return jnp.pad(whole, ((0, -whole.shape[0] % unit), (0, 0)))

    tail_own = pack(qkv_grad_own, out_grad[0], qkv_sum_own, up_sum_own)
    tail_par = pack(qkv_grad_par, out_grad[1], qkv_sum_par, up_sum_par)
    tail_sum = reduce_all(add_pair(tail_own, swap(tail_par)))

    shares = d_hidden_glob.reshape(group_size, 2, own_glob, dim)
    kept = lax.dynamic_index_in_dim(shares, tp_pos, 1, keepdims=False)
    sent = lax.dynamic_index_in_dim(shares, 1 - tp_pos, 1, keepdims=False)
    current = add_pair(kept, swap(sent))
    for bit in reversed(range(group_bits)):
        count = current.shape[0] // 2
        side = (group_pos >> bit) & 1
        sent = lax.dynamic_slice_in_dim(current, (1 - side) * count, count, 0)
        kept = lax.dynamic_slice_in_dim(current, side * count, count, 0)
        received = flip(sent, bit)
        if bit:
            current = add_pair(kept, received)
    d_mid_own = lax.dynamic_slice_in_dim(d_mid, rows + own_first, own_glob, 0)
    glob_grad = glob_input(kept[0], received[0], glob_tokens, d_mid_own, gain_a)

    out_tokens = (middle[:rows] + add_par[:rows] + add_own[:rows] + b_down).astype(BF16)

    def own_rows(array_in):
        return lax.dynamic_slice_in_dim(array_in, rows + own_first, own_glob, 0)

    out_glob = (own_rows(middle) + own_rows(add_par) + own_rows(add_own) + b_down).astype(BF16)
    units = w_up.shape[1]
    chunks = units // TILE
    ffn_sum = ffn_sum.reshape(chunks, -1, LANES)
    cut = TILE * dim // LANES
    up_grad = (
        ffn_sum[:, :cut]
        .reshape(chunks, TILE // LANES, dim, LANES)
        .transpose(2, 0, 1, 3)
        .reshape(dim, units)
        .astype(F32)
    )
    down_grad = (
        ffn_sum[:, cut:]
        .reshape(chunks, dim // LANES, TILE, LANES)
        .transpose(0, 2, 1, 3)
        .reshape(units, dim)
        .astype(F32)
    )
    count = 3 * half * dim // LANES
    qkv_all = (
        tail_sum[:count].reshape(3, half // LANES, dim, LANES).transpose(0, 2, 1, 3).astype(F32)
    ).reshape(3, dim, half)
    out_all = (
        tail_sum[count : count + half * dim // LANES]
        .reshape(dim // LANES, half, LANES)
        .transpose(1, 0, 2)
        .reshape(half, dim)
        .astype(F32)
    )
    small = tail_sum[count + half * dim // LANES :].reshape(-1).astype(F32)
    shared = small[: 6 * dim]
    shared = jnp.where(tp_pos == 0, shared, swap(shared))
    gain_f_grad, shift_f_grad, out_bias, down_bias, gain_a_grad, shift_a_grad = (
        shared.reshape(6, dim)
    )
    b_query_grad = small[6 * dim : 6 * dim + half]
    b_value_grad = small[6 * dim + half : 6 * dim + 2 * half]
    b_up_grad = small[6 * dim + 2 * half : 6 * dim + 2 * half + units]
    return (
        out_tokens, out_glob, tokens_grad, glob_grad, qkv_all[0], b_query_grad, qkv_all[1],
        qkv_all[2], b_value_grad, out_all, out_bias, up_grad, b_up_grad, down_grad, down_bias,
        gain_a_grad, shift_a_grad, gain_f_grad, shift_f_grad,
    )


def solution(mesh):
    rows = P(("seq", "tp"), None)
    cols, part, whole = P(None, "tp"), P("tp"), P()
    lines = P("tp", None)
    return jax.shard_map(
        per_device,
        mesh=mesh,
        in_specs=(
            rows, rows, cols, part, cols, cols, part, lines, whole, cols, part, lines, whole,
            whole, whole, whole, whole, whole, whole, rows, rows,
        ),
        out_specs=(
            rows, rows, rows, rows, cols, part, cols, cols, part, lines, whole, cols, part, lines,
            whole, whole, whole, whole, whole,
        ),
        check_vma=False,
    )
```

time: 1090 us -> 594 us (0.54)
  matrix products: 224 us -> 0 us
  Pallas kernels: 0 us -> 223 us
  blocking collectives: 207 us -> 0 us
  waiting for transfers between devices: 359 us -> 152 us
  local copies, waits for them, and re-layouts: 186 us -> 83.6 us
  other arithmetic: 62.2 us -> 91.3 us
  starting transfers between devices: 14.9 us -> 31.6 us
  loops' own time: 14.4 us -> 0 us
  between operations: 16.1 us -> 1.84 us
    psum x1 -> x0, waiting for transfers between devices: 264 us -> none  [per_device(): lax.psum((w_query_grad, b_query_grad, w_key_grad, w_value_grad, b_value_g...]
    dot_general x85 -> x0, matrix products: 224 us -> none  [the longest x6 53.8 us: mat_prod(): return jnp.dot(left, right, preferred_element_type=jnp.float32)]
    pallas_call x0 -> x18, Pallas kernels: none -> 223 us  [the longest x2 75.6 us: ffn_half(): pl.pallas_call(ffn_body, grid=(steps,), in_specs=[full(hidden.shape), ful...]
    psum x3 -> x0, blocking collectives: 199 us -> none  [the longest x1 78.8 us: per_device(): lax.psum((w_query_grad, b_query_grad, w_key_grad, w_value_grad, b_value_g...]
    ppermute x12 -> x37, waiting for transfers between devices: 27.5 us -> 152 us  [the longest x16 104 us: trade(): return lax.ppermute(value, ('seq', 'tp'), links)]
    reduce_sum x27 -> x0, other arithmetic: 48.7 us -> none  [the longest x6 13 us: norm_rows(): return centred * lax.rsqrt(row_var + EPS) * gain_vec + shift_vec]
    all_gather x4 -> x0, waiting for transfers between devices: 39.2 us -> none  [pair_gather(): lax.all_gather(tok_part, 'tp', axis=0, tiled=True)]
    select_n x7 -> x15, other arithmetic: 0.86 us -> 36.3 us  [the longest x8 33.8 us: reduce_all(): jnp.where(side, jnp.concatenate([other, value], 0), jnp.concatenate([valu...]
  transfers between devices with their start and end apart: 25 -> 37, of which waited for: 17 -> 17; matrix products, arithmetic and copies ran while one was open for 15% -> 19% of each run, Pallas kernels for 0% -> 13%
where the time goes in v1:
time: 594 us; the launch traced here: 584 us
  Pallas kernels  223 us (38%)
  waiting for transfers between devices  152 us (26%)
  other arithmetic  91.3 us (15%)
  local copies, waits for them, and re-layouts  83.6 us (14%)
  starting transfers between devices  31.6 us (5%)
    ppermute x16, waiting for transfers between devices, trade(): return lax.ppermute(value, ('seq', 'tp'), links)  104 us
    pallas_call x2, Pallas kernels, ffn_half(): pl.pallas_call(ffn_body, grid=(steps,), in_specs=[full(hidden.shape), ful...  75.6 us
    unnamed x89, local copies, waits for them, and re-layouts  40.4 us
    ppermute x9, waiting for transfers between devices, flip(): lax.ppermute(value, 'seq', [(s, s ^ 1 << bit) for s in range(seq_size)])  40 us
    pallas_call x1, Pallas kernels, attention_back(): pl.pallas_call(attention_back_body, grid_spec=pltpu.PrefetchScalarGridSpe...  35.1 us
    select_n x8, other arithmetic, reduce_all(): jnp.where(side, jnp.concatenate([other, value], 0), jnp.concatenate([valu...  33.8 us
    pallas_call x1, Pallas kernels, local_forward(): pl.pallas_call(local_forward_body, grid_spec=pltpu.PrefetchScalarGridSpec...  23.2 us
    convert_element_type x13, other arithmetic, add_pair(): return (own.astype(F32) + received.astype(F32)).astype(BF16)  19.8 us
  transfers between devices with their start and end apart: 37, of which 17 were waited for; matrix products, arithmetic and copies ran while one was open for 19% of the time, Pallas kernels for 13%

profile of v1, /device:TPU:0, one launch (start us, length us, event | category | flops | bytes accessed | tf_op | source)
XLA Modules:
  0.0 583.9 jit_solution(7369664776261605437)
XLA Ops:
  16.5 3.3 select_convert_fusion.augk_ref
  36.1 3.4 collective-permute-done.2
  45.8 9.1 %project.2 = (bf16[1280,2304]{1,0:T(8,128)(2,1)}, bf16[768,1280]{1,0:T(8,128)(2,1)}) custom-call(bf16[1024,768]{1,0:T(8,128)(2,1)} %x_ref.6, f32[1,768]{1,0:T(1,128)} %reshape.387.gain_ref, f32[1,768]{1,0:T(1,128)} %reshape.388.shift_ref, bf16[768,1152]{1,0:T(8,128)(2,1)} %copy-done.6, bf16[768,1152]{1,0:T(8,128)(2,1)} %copy-done.8, ...), custom_call_target="tpu_custom_call" | custom-call | flops 3623878656 | bytes 11403264 | tf_op jit(solution)/shard_map/project/pallas_call | solution.py:112
  54.9 4.7 project.3
  59.6 13.3 %glob_forward.1 = bf16[12,80,256]{2,1,0:T(8,128)(2,1)} custom-call(bf16[1280,2304]{1,0:T(8,128)(2,1)} %get-tuple-element.62.q_ref.k_ref.v_ref.kg_ref.vg_ref, bf16[1280,2304]{1,0:T(8,128)(2,1)} %get-tuple-element.62.q_ref.k_ref.v_ref.kg_ref.vg_ref, bf16[1280,2304]{1,0:T(8,128)(2,1)} %get-tuple-element.62.q_ref.k_ref.v_ref.kg_ref.vg_ref, ...), custom_call_target="tpu_custom_call" | custom-call | flops 4026531840 | bytes 5898240 | tf_op jit(solution)/shard_map/glob_forward/pallas_call | solution.py:173
  79.8 7.8 %collective-permute-done.7.right_ref = bf16[6,80,256]{2,1,0:T(8,128)(2,1)S(1)} collective-permute-done((bf16[6,80,256]{2,1,0:T(8,128)(2,1)}, bf16[6,80,256]{2,1,0:T(8,128)(2,1)S(1)}, u32[]{:S(2)}, u32[]{:S(2)}) %collective-permute-start.7) | collective-permute-done | bytes 245792 | tf_op jit(solution)/shard_map/ppermute | solution.py:808
  103.4 4.6 collective-permute-done.9.right_ref
  110.7 23.2 %local_forward.1 = (bf16[1280,768]{1,0:T(8,128)(2,1)}, bf16[1280,768]{1,0:T(8,128)(2,1)}, bf16[768,1280]{1,0:T(8,128)(2,1)}, f32[2,6,2,512]{3,2,1,0:T(2,128)}) custom-call(s32[2]{0:T(128)} %copy-done.30, bf16[1280,2304]{1,0:T(8,128)(2,1)} %get-tuple-element.62.q_ref.k_ref.v_ref.kg_ref.vg_ref, ...), custom_call_target="tpu_custom_call" | custom-call | flops 8053063680 | bytes 5898240 | tf_op jit(solution)/shard_map/local_forward/pallas_call | solution.py:260
  134.8 7.1 %middle_local.1 = (f32[1280,768]{1,0:T(8,128)}, bf16[1280,768]{1,0:T(8,128)(2,1)}, bf16[768,1280]{1,0:T(8,128)(2,1)}) custom-call(bf16[1280,768]{1,0:T(8,128)(2,1)} %get-tuple-element.63.out_ref.rest_3_, bf16[1024,768]{1,0:T(8,128)(2,1)} %x_ref.6, bf16[384,768]{1,0:T(8,128)(2,1)} %own_ref.5, bf16[384,768]{1,0:T(8,128)(2,1)} %copy-done.5, ...), custom_call_target="tpu_custom_call" | custom-call | flops 1207959552 | bytes 10616832 | tf_op jit(solution)/shard_map/middle_local/pallas_call | solution.py:317
  142.6 3.4 middle_glob.1
  145.9 37.9 %ffn_half.3 = (f32[1280,768]{1,0:T(8,128)}, f32[1280,768]{1,0:T(8,128)}, bf16[6,3072,128]{2,1,0:T(8,128)(2,1)}, f32[1,1536]{1,0:T(1,128)}) custom-call(bf16[1280,768]{1,0:T(8,128)(2,1)} %get-tuple-element.70.hid_ref, bf16[768,1280]{1,0:T(8,128)(2,1)} %get-tuple-element.71.turned_ref, bf16[1280,768]{1,0:T(8,128)(2,1)} %pad_maximum_fusion.dz_ref, ...), custom_call_target="tpu_custom_call" | custom-call | flops 18119393280 | bytes 23199744 | tf_op jit(solution)/shard_map/ffn_half/pallas_call | solution.py:439
  183.8 37.7 %ffn_half.2 = (f32[1280,768]{1,0:T(8,128)}, f32[1280,768]{1,0:T(8,128)}, bf16[6,3072,128]{2,1,0:T(8,128)(2,1)}, f32[1,1536]{1,0:T(1,128)}) custom-call(bf16[1280,768]{1,0:T(8,128)(2,1)} %get-tuple-element.70.hid_ref, bf16[768,1280]{1,0:T(8,128)(2,1)} %get-tuple-element.71.turned_ref, bf16[1280,768]{1,0:T(8,128)(2,1)} %pad_maximum_fusion.dz_ref, ...), custom_call_target="tpu_custom_call" | custom-call | flops 18119393280 | bytes 23199744 | tf_op jit(solution)/shard_map/ffn_half/pallas_call | solution.py:439
  221.6 15.6 %middle_back.1 = (f32[1280,768]{1,0:T(8,128)}, bf16[1280,768]{1,0:T(8,128)(2,1)}, f32[16,1280]{1,0:T(8,128)}, bf16[2,2304,128]{2,1,0:T(8,128)(2,1)}, f32[8,768]{1,0:T(8,128)}) custom-call(f32[1280,768]{1,0:T(8,128)} %get-tuple-element.74.dn_one_ref, f32[1280,768]{1,0:T(8,128)} %get-tuple-element.75.dn_two_ref, f32[1280,768]{1,0:T(8,128)} %get-tuple-element.69.mid_ref, ...), custom_call_target="tpu_custom_call" | custom-call | flops 3019898880 | bytes 27525120 | tf_op jit(solution)/shard_map/middle_back/pallas_call | solution.py:531
  237.2 35.1 %attention_back.1 = (bf16[1280,768]{1,0:T(8,128)(2,1)}, bf16[1280,768]{1,0:T(8,128)(2,1)}, bf16[1280,768]{1,0:T(8,128)(2,1)}) custom-call(s32[2]{0:T(128)} %copy-done.30, bf16[1280,2304]{1,0:T(8,128)(2,1)} %get-tuple-element.62.q_ref.k_ref.v_ref.kg_ref.vg_ref, bf16[1280,2304]{1,0:T(8,128)(2,1)} %get-tuple-element.62.q_ref.k_ref.v_ref.kg_ref.vg_ref, ...), custom_call_target="tpu_custom_call" | custom-call | flops 30198988800 | bytes 11796480 | tf_op jit(solution)/shard_map/attention_back/pallas_call | solution.py:634
  272.3 7.0 %project_grad.3 = (bf16[9,768,128]{2,1,0:T(8,128)(2,1)}, f32[8,384]{1,0:T(8,128)}) custom-call(bf16[768,1280]{1,0:T(8,128)(2,1)} %get-tuple-element.89.turned_ref, bf16[1280,768]{1,0:T(8,128)(2,1)} %get-tuple-element.83.dq_ref, bf16[1280,768]{1,0:T(8,128)(2,1)} %get-tuple-element.84.dk_ref, bf16[1280,768]{1,0:T(8,128)(2,1)} %get-tuple-element.85.dv_ref), custom_call_target="tpu_custom_call" | custom-call | flops 2264924160 | bytes 4915200 | tf_op jit(solution)/shard_map/project_grad/pallas_call | solution.py:686
  279.2 6.8 %project_grad.2 = (bf16[9,768,128]{2,1,0:T(8,128)(2,1)}, f32[8,384]{1,0:T(8,128)}) custom-call(bf16[768,1280]{1,0:T(8,128)(2,1)} %get-tuple-element.89.turned_ref, bf16[1280,768]{1,0:T(8,128)(2,1)} %get-tuple-element.83.dq_ref, bf16[1280,768]{1,0:T(8,128)(2,1)} %get-tuple-element.84.dk_ref, bf16[1280,768]{1,0:T(8,128)(2,1)} %get-tuple-element.85.dv_ref), custom_call_target="tpu_custom_call" | custom-call | flops 2264924160 | bytes 4915200 | tf_op jit(solution)/shard_map/project_grad/pallas_call | solution.py:686
  286.1 13.1 %input_back.1 = (f32[1024,768]{1,0:T(8,128)}, bf16[256,768]{1,0:T(8,128)(2,1)}, f32[8,768]{1,0:T(8,128)}) custom-call(bf16[1280,768]{1,0:T(8,128)(2,1)} %get-tuple-element.83.dq_ref, bf16[1280,768]{1,0:T(8,128)(2,1)} %get-tuple-element.84.dk_ref, bf16[1280,768]{1,0:T(8,128)(2,1)} %get-tuple-element.85.dv_ref, bf16[768,1152]{1,0:T(8,128)(2,1)} %copy-done.6, ...), custom_call_target="tpu_custom_call" | custom-call | flops 4529848320 | bytes 19267584 | tf_op jit(solution)/shard_map/input_back/pallas_call | solution.py:741
  301.0 11.5 %fusion.9 = bf16[9472,128]{1,0:T(8,128)(2,1)S(1)} fusion(bf16[54,128]{1,0:T(8,128)(2,1)S(1)} %get-tuple-element.186, bf16[2304,128]{1,0:T(8,128)(2,1)S(1)} %get-tuple-element.170, bf16[6912,128]{1,0:T(8,128)(2,1)} %bitcast.97), kind=kLoop, calls=%fused_computation.19 | loop fusion | flops 12124160 | bytes 4797952 | tf_op jit(solution)/shard_map/concatenate | solution.py:958
  313.1 7.0 %collective-permute-done.18 = bf16[9472,128]{1,0:T(8,128)(2,1)} collective-permute-done((bf16[9472,128]{1,0:T(8,128)(2,1)S(1)}, bf16[9472,128]{1,0:T(8,128)(2,1)}, u32[]{:S(2)}, u32[]{:S(2)}) %collective-permute-start.18) | collective-permute-done | bytes 2424864 | tf_op jit(solution)/shard_map/ppermute | solution.py:811
  320.1 11.6 %add_convert_fusion.1 = bf16[9472,128]{1,0:T(8,128)(2,1)S(1)} fusion(bf16[9472,128]{1,0:T(8,128)(2,1)} %collective-permute-done.18, bf16[54,128]{1,0:T(8,128)(2,1)S(1)} %get-tuple-element.185, bf16[2304,128]{1,0:T(8,128)(2,1)S(1)} %get-tuple-element.169, bf16[6912,128]{1,0:T(8,128)(2,1)} %bitcast.96), kind=kLoop, calls=%fused_computation.8 | loop fusion | flops 15761408 | bytes 7222784 | tf_op jit(solution)/shard_map/convert_element_type | solution.py:907
  333.3 3.6 add_convert_fusion
  341.4 8.3 %collective-permute-done.19 = bf16[4736,128]{1,0:T(8,128)(2,1)} collective-permute-done((bf16[4736,128]{1,0:T(8,128)(2,1)}, bf16[4736,128]{1,0:T(8,128)(2,1)}, u32[]{:S(2)}, u32[]{:S(2)}) %collective-permute-start.19) | collective-permute-done | bytes 1212448 | tf_op jit(solution)/shard_map/ppermute | solution.py:918
  352.0 29.4 %collective-permute-done.29 = bf16[9216,128]{1,0:T(8,128)(2,1)} collective-permute-done((bf16[9216,128]{1,0:T(8,128)(2,1)}, bf16[9216,128]{1,0:T(8,128)(2,1)}, u32[]{:S(2)}, u32[]{:S(2)}) %collective-permute-start.29) | collective-permute-done | bytes 2359328 | tf_op jit(solution)/shard_map/ppermute | solution.py:918
  385.5 4.0 add_convert_fusion.3
  391.3 8.6 %collective-permute-done.30 = bf16[4608,128]{1,0:T(8,128)(2,1)S(1)} collective-permute-done((bf16[4608,128]{1,0:T(8,128)(2,1)S(1)}, bf16[4608,128]{1,0:T(8,128)(2,1)S(1)}, u32[]{:S(2)}, u32[]{:S(2)}) %collective-permute-start.30) | collective-permute-done | bytes 1179680 | tf_op jit(solution)/shard_map/ppermute | solution.py:918
  402.0 2.7 collective-permute-start.22
  404.7 12.8 %collective-permute-done.31 = bf16[2304,128]{1,0:T(8,128)(2,1)S(1)} collective-permute-done((bf16[2304,128]{1,0:T(8,128)(2,1)S(1)}, bf16[2304,128]{1,0:T(8,128)(2,1)S(1)}, u32[]{:S(2)}, u32[]{:S(2)}) %collective-permute-start.31) | collective-permute-done | bytes 589856 | tf_op jit(solution)/shard_map/ppermute | solution.py:918
  420.9 16.1 %collective-permute-done.32 = bf16[1152,128]{1,0:T(8,128)(2,1)S(1)} collective-permute-done((bf16[1152,128]{1,0:T(8,128)(2,1)S(1)}, bf16[1152,128]{1,0:T(8,128)(2,1)S(1)}, u32[]{:S(2)}, u32[]{:S(2)}) %collective-permute-start.32) | collective-permute-done | bytes 294944 | tf_op jit(solution)/shard_map/ppermute | solution.py:918
  439.3 6.1 %collective-permute-done.23 = bf16[592,128]{1,0:T(8,128)(2,1)S(1)} collective-permute-done((bf16[592,128]{1,0:T(8,128)(2,1)S(1)}, bf16[592,128]{1,0:T(8,128)(2,1)S(1)}, u32[]{:S(2)}, u32[]{:S(2)}) %collective-permute-start.23) | collective-permute-done | bytes 151584 | tf_op jit(solution)/shard_map/ppermute | solution.py:918
  445.5 5.9 %collective-permute-done.33 = bf16[1152,128]{1,0:T(8,128)(2,1)S(1)} collective-permute-done((bf16[1152,128]{1,0:T(8,128)(2,1)S(1)}, bf16[1152,128]{1,0:T(8,128)(2,1)S(1)}, u32[]{:S(2)}, u32[]{:S(2)}) %collective-permute-start.33) | collective-permute-done | bytes 294944 | tf_op jit(solution)/shard_map/ppermute | solution.py:918
  452.5 5.4 collective-permute-done.24
  458.7 11.5 %collective-permute-done.34 = bf16[2304,128]{1,0:T(8,128)(2,1)S(1)} collective-permute-done((bf16[2304,128]{1,0:T(8,128)(2,1)S(1)}, bf16[2304,128]{1,0:T(8,128)(2,1)S(1)}, u32[]{:S(2)}, u32[]{:S(2)}) %collective-permute-start.34) | collective-permute-done | bytes 589856 | tf_op jit(solution)/shard_map/ppermute | solution.py:918
  478.1 21.1 %collective-permute-done.17 = bf16[1,16,768]{2,1,0:T(8,128)(2,1)S(1)} collective-permute-done((bf16[1,16,768]{2,1,0:T(8,128)(2,1)S(1)}, bf16[1,16,768]{2,1,0:T(8,128)(2,1)S(1)}, u32[]{:S(2)}, u32[]{:S(2)}) %collective-permute-start.17) | collective-permute-done | bytes 24608 | tf_op jit(solution)/shard_map/ppermute | solution.py:808
  501.5 9.5 %maximum_select_fusion.2 = bf16[9216,128]{1,0:T(8,128)(2,1)S(1)} fusion(bf16[4608,128]{1,0:T(8,128)(2,1)S(1)} %maximum_select_fusion.4, bf16[4608,128]{1,0:T(8,128)(2,1)} %collective-permute-done.35, pred[]{:T(512)S(6)} %eq.139), kind=kLoop, calls=%fused_computation.22 | loop fusion | flops 10616832 | bytes 4718593 | tf_op jit(solution)/shard_map/jit(_where)/select_n | solution.py:934
  511.7 4.4 maximum_select_fusion.1
  522.4 2.7 copy.81
  525.0 2.7 copy.87
  527.7 2.7 copy.80
  530.3 2.7 copy.86
  533.0 2.7 copy.79
  535.6 2.7 copy.85
  539.7 2.7 copy.84
  543.7 17.9 %maximum_select_fusion = bf16[18432,128]{1,0:T(8,128)(2,1)S(1)} fusion(bf16[9216,128]{1,0:T(8,128)(2,1)S(1)} %maximum_select_fusion.2, bf16[9216,128]{1,0:T(8,128)(2,1)} %collective-permute-done.36, pred[]{:T(512)S(6)} %eq.138), kind=kLoop, calls=%fused_computation.10 | loop fusion | flops 21233664 | bytes 9437185 | tf_op jit(solution)/shard_map/jit(_where)/select_n | solution.py:934
  561.9 2.6 convert_bitcast_fusion.1
  564.5 6.1 %copy.82 = f32[768,6,2,128]{0,3,2,1:T(8,128)} copy(f32[768,6,2,128]{3,0,2,1:T(8,128)} %convert_bitcast_fusion.1) | data formatting | bytes 9437184 | tf_op jit(solution)/shard_map/convert_element_type | solution.py:996
  570.6 6.3 %copy.88 = f32[768,1536]{1,0:T(8,128)} copy(f32[768,1536]{0,1:T(8,128)} %bitcast.81) | data formatting | bytes 9437184
  577.4 2.8 copy.83
  580.2 3.3 copy.94
  (250 shorter events, 112.2 us)
Async XLA Ops:
  2.1 32.7 %collective-permute-start.5 = (f32[2304]{0:T(1024)}, f32[2304]{0:T(1024)}, u32[]{:S(2)}, u32[]{:S(2)}) collective-permute-start(f32[2304]{0:T(1024)} %pad_maximum_fusion.3), channel_id=1, source_target_pairs={{0,1},{1,0},{2,3},{3,2},{4,5},{5,4},{6,7},{7,6},{8,9},{9,8},{10,11... | collective-permute-start | bytes 27656 | tf_op jit(solution)/shard_map/ppermute | solution.py:811
  3.9 23.3 %collective-permute-start = (bf16[1,2,16,768]{3,2,1,0:T(8,128)(2,1)}, bf16[1,2,16,768]{3,2,1,0:T(8,128)(2,1)}, u32[]{:S(2)}, u32[]{:S(2)}) collective-permute-start(bf16[1,2,16,768]{3,2,1,0:T(8,128)(2,1)} %maximum_bitcast_fusion), channel_id=1, source_target_pairs={{0,2},{2,0},{4,6},{6,4},{8,10},{10,8},{12,14},{14,12},{16,18},{18,... | collective-permute-start | bytes 147464 | tf_op jit(solution)/shard_map/ppermute | solution.py:808
  8.8 35.0 %copy-start.6 = (bf16[768,1152]{1,0:T(8,128)(2,1)}, bf16[768,1152]{1,0:T(8,128)(2,1)S(1)}, u32[]{:S(2)}) copy-start(bf16[768,1152]{1,0:T(8,128)(2,1)S(1)} %constant_dynamic-update-slice_fusion.own_ref) | copy-start | bytes 5308420
  8.8 35.8 %collective-permute-start.4 = (bf16[768,1152]{1,0:T(8,128)(2,1)S(1)}, bf16[768,1152]{1,0:T(8,128)(2,1)S(1)}, u32[]{:S(2)}, u32[]{:S(2)}) collective-permute-start(bf16[768,1152]{1,0:T(8,128)(2,1)S(1)} %constant_dynamic-update-slice_fusion.own_ref), channel_id=1, source_target_pairs={{0,1},{1,0},{2,3},{3,2},{4,5},{5,4},{6,7},{7,6},{8,9},{9,8},{10,11... | collective-permute-start | bytes 5308424 | tf_op jit(solution)/shard_map/ppermute | solution.py:811
  28.1 5.0 collective-permute-start.1
  33.1 6.3 %collective-permute-start.2 = (bf16[4,2,16,768]{3,2,1,0:T(8,128)(2,1)S(1)}, bf16[4,2,16,768]{3,2,1,0:T(8,128)(2,1)S(1)}, u32[]{:S(2)}, u32[]{:S(2)}) collective-permute-start(bf16[4,2,16,768]{3,2,1,0:T(8,128)(2,1)S(1)} %maximum_select_fusion.11), channel_id=1, source_target_pairs={{0,8},{2,10},{4,12},{6,14},{8,0},{10,2},{12,4},{14,6},{16,24},{18,... | collective-permute-start | bytes 589832 | tf_op jit(solution)/shard_map/ppermute | solution.py:808
  39.5 4.1 collective-permute-start.3
  59.6 32.2 %copy-start.32 = (bf16[768,1536]{1,0:T(8,128)(2,1)S(1)}, bf16[768,1536]{1,0:T(8,128)(2,1)}, u32[]{:S(2)}) copy-start(bf16[768,1536]{1,0:T(8,128)(2,1)} %up_ref.1) | copy-start | bytes 7077892
  72.9 18.8 %copy-start.4 = (bf16[384,768]{1,0:T(8,128)(2,1)S(1)}, bf16[384,768]{1,0:T(8,128)(2,1)}, u32[]{:S(2)}) copy-start(bf16[384,768]{1,0:T(8,128)(2,1)} %own_ref.5) | copy-start | bytes 1769476
  72.9 19.4 %copy-start.20 = (f32[1536]{0:T(1024)S(1)}, f32[1536]{0:T(1024)}, u32[]{:S(2)}) copy-start(f32[1536]{0:T(1024)} %param.32) | copy-start | bytes 18436
  72.9 20.0 %copy-start.27 = (f32[768]{0:T(1024)S(1)}, f32[768]{0:T(1024)}, u32[]{:S(2)}) copy-start(f32[768]{0:T(1024)} %param.37) | copy-start | bytes 9220
  72.9 20.6 %copy-start.28 = (f32[768]{0:T(1024)S(1)}, f32[768]{0:T(1024)}, u32[]{:S(2)}) copy-start(f32[768]{0:T(1024)} %param.30) | copy-start | bytes 9220
  72.9 21.2 %copy-start.29 = (f32[768]{0:T(1024)S(1)}, f32[768]{0:T(1024)}, u32[]{:S(2)}) copy-start(f32[768]{0:T(1024)} %param.38) | copy-start | bytes 9220
  72.9 29.1 %copy-start.9 = (bf16[1024,768]{1,0:T(8,128)(2,1)S(1)}, bf16[1024,768]{1,0:T(8,128)(2,1)}, u32[]{:S(2)}) copy-start(bf16[1024,768]{1,0:T(8,128)(2,1)} %param.41) | copy-start | bytes 4718596
  74.9 1.6 collective-permute-start.6
  79.1 8.4 %collective-permute-start.7 = (bf16[6,80,256]{2,1,0:T(8,128)(2,1)}, bf16[6,80,256]{2,1,0:T(8,128)(2,1)S(1)}, u32[]{:S(2)}, u32[]{:S(2)}) collective-permute-start(bf16[6,80,256]{2,1,0:T(8,128)(2,1)} %merge.4.left_ref), channel_id=1, source_target_pairs={{0,2},{2,0},{4,6},{6,4},{8,10},{10,8},{12,14},{14,12},{16,18},{18,... | collective-permute-start | bytes 737288 | tf_op jit(solution)/shard_map/ppermute | solution.py:808
  90.2 7.6 %collective-permute-start.8 = (bf16[6,80,256]{2,1,0:T(8,128)(2,1)}, bf16[6,80,256]{2,1,0:T(8,128)(2,1)S(1)}, u32[]{:S(2)}, u32[]{:S(2)}) collective-permute-start(bf16[6,80,256]{2,1,0:T(8,128)(2,1)} %merge.5.left_ref), channel_id=1, source_target_pairs={{0,4},{2,6},{4,0},{6,2},{8,12},{10,14},{12,8},{14,10},{16,20},{18,... | collective-permute-start | bytes 737288 | tf_op jit(solution)/shard_map/ppermute | solution.py:808
  91.7 42.2 %collective-permute-start.11 = (bf16[384,768]{1,0:T(8,128)(2,1)S(1)}, bf16[384,768]{1,0:T(8,128)(2,1)S(1)}, u32[]{:S(2)}, u32[]{:S(2)}) collective-permute-start(bf16[384,768]{1,0:T(8,128)(2,1)S(1)} %copy-done.4), channel_id=1, source_target_pairs={{0,1},{1,0},{2,3},{3,2},{4,5},{5,4},{6,7},{7,6},{8,9},{9,8},{10,11... | collective-permute-start | bytes 1769480 | tf_op jit(solution)/shard_map/ppermute | solution.py:811
  91.7 92.1 %collective-permute-start.12 = (bf16[768,1536]{1,0:T(8,128)(2,1)S(1)}, bf16[768,1536]{1,0:T(8,128)(2,1)}, u32[]{:S(2)}, u32[]{:S(2)}) collective-permute-start(bf16[768,1536]{1,0:T(8,128)(2,1)S(1)} %copy-done.32), channel_id=1, source_target_pairs={{0,1},{1,0},{2,3},{3,2},{4,5},{5,4},{6,7},{7,6},{8,9},{9,8},{10,11... | collective-permute-start | bytes 7077896 | tf_op jit(solution)/shard_map/ppermute | solution.py:811
  92.2 91.6 %collective-permute-start.13 = (bf16[1536,768]{1,0:T(8,128)(2,1)}, bf16[1536,768]{1,0:T(8,128)(2,1)}, u32[]{:S(2)}, u32[]{:S(2)}) collective-permute-start(bf16[1536,768]{1,0:T(8,128)(2,1)} %down_ref.1), channel_id=1, source_target_pairs={{0,1},{1,0},{2,3},{3,2},{4,5},{5,4},{6,7},{7,6},{8,9},{9,8},{10,11... | collective-permute-start | bytes 7077896 | tf_op jit(solution)/shard_map/ppermute | solution.py:811
  100.5 7.6 %collective-permute-start.9 = (bf16[6,80,256]{2,1,0:T(8,128)(2,1)}, bf16[6,80,256]{2,1,0:T(8,128)(2,1)S(1)}, u32[]{:S(2)}, u32[]{:S(2)}) collective-permute-start(bf16[6,80,256]{2,1,0:T(8,128)(2,1)} %merge.6.left_ref), channel_id=1, source_target_pairs={{0,8},{2,10},{4,12},{6,14},{8,0},{10,2},{12,4},{14,6},{16,24},{18,... | collective-permute-start | bytes 737288 | tf_op jit(solution)/shard_map/ppermute | solution.py:808
  110.7 31.2 %collective-permute-start.10 = (bf16[6,80,256]{2,1,0:T(8,128)(2,1)}, bf16[6,80,256]{2,1,0:T(8,128)(2,1)S(1)}, u32[]{:S(2)}, u32[]{:S(2)}) collective-permute-start(bf16[6,80,256]{2,1,0:T(8,128)(2,1)} %merge.7.own_out_ref), channel_id=1, source_target_pairs={{0,1},{1,0},{2,3},{3,2},{4,5},{5,4},{6,7},{7,6},{8,9},{9,8},{10,11... | collective-permute-start | bytes 737288 | tf_op jit(solution)/shard_map/ppermute | solution.py:811
  286.1 13.9 %copy-start.25 = (f32[1,1536]{1,0:T(1,128)S(1)}, f32[1,1536]{1,0:T(1,128)}, u32[]{:S(2)}) copy-start(f32[1,1536]{1,0:T(1,128)} %get-tuple-element.95) | copy-start | bytes 18436
  286.1 14.7 %copy-start.10 = (bf16[2,2304,128]{2,1,0:T(8,128)(2,1)S(1)}, bf16[2,2304,128]{2,1,0:T(8,128)(2,1)}, u32[]{:S(2)}) copy-start(bf16[2,2304,128]{2,1,0:T(8,128)(2,1)} %get-tuple-element.91) | copy-start | bytes 3538948
  312.5 7.6 %collective-permute-start.18 = (bf16[9472,128]{1,0:T(8,128)(2,1)S(1)}, bf16[9472,128]{1,0:T(8,128)(2,1)}, u32[]{:S(2)}, u32[]{:S(2)}) collective-permute-start(bf16[9472,128]{1,0:T(8,128)(2,1)S(1)} %fusion.9), channel_id=1, source_target_pairs={{0,1},{1,0},{2,3},{3,2},{4,5},{5,4},{6,7},{7,6},{8,9},{9,8},{10,11... | collective-permute-start | bytes 7274504 | tf_op jit(solution)/shard_map/ppermute | solution.py:811
  313.0 20.3 %collective-permute-start.28 = (bf16[6,3072,128]{2,1,0:T(8,128)(2,1)}, bf16[6,3072,128]{2,1,0:T(8,128)(2,1)}, u32[]{:S(2)}, u32[]{:S(2)}) collective-permute-start(bf16[6,3072,128]{2,1,0:T(8,128)(2,1)} %get-tuple-element.100), channel_id=1, source_target_pairs={{0,1},{1,0},{2,3},{3,2},{4,5},{5,4},{6,7},{7,6},{8,9},{9,8},{10,11... | collective-permute-start | bytes 14155784 | tf_op jit(solution)/shard_map/ppermute | solution.py:811
  332.8 16.9 %collective-permute-start.19 = (bf16[4736,128]{1,0:T(8,128)(2,1)}, bf16[4736,128]{1,0:T(8,128)(2,1)}, u32[]{:S(2)}, u32[]{:S(2)}) collective-permute-start(bf16[4736,128]{1,0:T(8,128)(2,1)} %constant_dynamic-slice_fusion.6), channel_id=1, source_target_pairs={{0,2},{2,0},{4,6},{6,4},{8,10},{10,8},{12,14},{14,12},{16,18},{18,... | collective-permute-start | bytes 3637256 | tf_op jit(solution)/shard_map/ppermute | solution.py:918
  339.8 41.6 %collective-permute-start.29 = (bf16[9216,128]{1,0:T(8,128)(2,1)}, bf16[9216,128]{1,0:T(8,128)(2,1)}, u32[]{:S(2)}, u32[]{:S(2)}) collective-permute-start(bf16[9216,128]{1,0:T(8,128)(2,1)} %constant_dynamic-slice_fusion.2), channel_id=1, source_target_pairs={{0,2},{2,0},{4,6},{6,4},{8,10},{10,8},{12,14},{14,12},{16,18},{18,... | collective-permute-start | bytes 7077896 | tf_op jit(solution)/shard_map/ppermute | solution.py:918
  341.3 40.1 %copy-start.2 = (bf16[6,3072,128]{2,1,0:T(8,128)(2,1)S(1)}, bf16[6,3072,128]{2,1,0:T(8,128)(2,1)}, u32[]{:S(2)}) copy-start(bf16[6,3072,128]{2,1,0:T(8,128)(2,1)} %copy-done.1) | copy-start | bytes 14155780
  341.3 78.1 %collective-permute-start.14 = (bf16[8,16,768]{2,1,0:T(8,128)(2,1)S(1)}, bf16[8,16,768]{2,1,0:T(8,128)(2,1)S(1)}, u32[]{:S(2)}, u32[]{:S(2)}) collective-permute-start(bf16[8,16,768]{2,1,0:T(8,128)(2,1)S(1)} %dynamic-slice_bitcast_fusion), channel_id=1, source_target_pairs={{0,1},{1,0},{2,3},{3,2},{4,5},{5,4},{6,7},{7,6},{8,9},{9,8},{10,11... | collective-permute-start | bytes 589832 | tf_op jit(solution)/shard_map/ppermute | solution.py:811
  351.3 38.1 %collective-permute-start.20 = (bf16[2368,128]{1,0:T(8,128)(2,1)S(1)}, bf16[2368,128]{1,0:T(8,128)(2,1)S(1)}, u32[]{:S(2)}, u32[]{:S(2)}) collective-permute-start(bf16[2368,128]{1,0:T(8,128)(2,1)S(1)} %constant_dynamic-slice_fusion.5), channel_id=1, source_target_pairs={{0,4},{2,6},{4,0},{6,2},{8,12},{10,14},{12,8},{14,10},{16,20},{18,... | collective-permute-start | bytes 1818632 | tf_op jit(solution)/shard_map/ppermute | solution.py:918
  383.6 16.3 %collective-permute-start.30 = (bf16[4608,128]{1,0:T(8,128)(2,1)S(1)}, bf16[4608,128]{1,0:T(8,128)(2,1)S(1)}, u32[]{:S(2)}, u32[]{:S(2)}) collective-permute-start(bf16[4608,128]{1,0:T(8,128)(2,1)S(1)} %constant_dynamic-slice_fusion.1), channel_id=1, source_target_pairs={{0,4},{2,6},{4,0},{6,2},{8,12},{10,14},{12,8},{14,10},{16,20},{18,... | collective-permute-start | bytes 3538952 | tf_op jit(solution)/shard_map/ppermute | solution.py:918
  389.7 12.3 %collective-permute-start.21 = (bf16[1184,128]{1,0:T(8,128)(2,1)S(1)}, bf16[1184,128]{1,0:T(8,128)(2,1)S(1)}, u32[]{:S(2)}, u32[]{:S(2)}) collective-permute-start(bf16[1184,128]{1,0:T(8,128)(2,1)S(1)} %constant_dynamic-slice_fusion.4), channel_id=1, source_target_pairs={{0,8},{2,10},{4,12},{6,14},{8,0},{10,2},{12,4},{14,6},{16,24},{18,... | collective-permute-start | bytes 909320 | tf_op jit(solution)/shard_map/ppermute | solution.py:918
  400.3 17.2 %collective-permute-start.31 = (bf16[2304,128]{1,0:T(8,128)(2,1)S(1)}, bf16[2304,128]{1,0:T(8,128)(2,1)S(1)}, u32[]{:S(2)}, u32[]{:S(2)}) collective-permute-start(bf16[2304,128]{1,0:T(8,128)(2,1)S(1)} %constant_dynamic-slice_fusion), channel_id=1, source_target_pairs={{0,8},{2,10},{4,12},{6,14},{8,0},{10,2},{12,4},{14,6},{16,24},{18,... | collective-permute-start | bytes 1769480 | tf_op jit(solution)/shard_map/ppermute | solution.py:918
  402.0 17.5 %collective-permute-start.22 = (bf16[592,128]{1,0:T(8,128)(2,1)S(1)}, bf16[592,128]{1,0:T(8,128)(2,1)S(1)}, u32[]{:S(2)}, u32[]{:S(2)}) collective-permute-start(bf16[592,128]{1,0:T(8,128)(2,1)S(1)} %constant_dynamic-slice_fusion.3), channel_id=1, source_target_pairs={{0,16},{2,18},{4,20},{6,22},{8,24},{10,26},{12,28},{14,30},{16,0},... | collective-permute-start | bytes 454664 | tf_op jit(solution)/shard_map/ppermute | solution.py:918
  417.7 19.3 %collective-permute-start.32 = (bf16[1152,128]{1,0:T(8,128)(2,1)S(1)}, bf16[1152,128]{1,0:T(8,128)(2,1)S(1)}, u32[]{:S(2)}, u32[]{:S(2)}) collective-permute-start(bf16[1152,128]{1,0:T(8,128)(2,1)S(1)} %constant_dynamic-slice_fusion.11), channel_id=1, source_target_pairs={{0,16},{2,18},{4,20},{6,22},{8,24},{10,26},{12,28},{14,30},{16,0},... | collective-permute-start | bytes 884744 | tf_op jit(solution)/shard_map/ppermute | solution.py:918
  419.6 25.8 %collective-permute-start.23 = (bf16[592,128]{1,0:T(8,128)(2,1)S(1)}, bf16[592,128]{1,0:T(8,128)(2,1)S(1)}, u32[]{:S(2)}, u32[]{:S(2)}) collective-permute-start(bf16[592,128]{1,0:T(8,128)(2,1)S(1)} %add_convert_fusion.10), channel_id=1, source_target_pairs={{0,16},{2,18},{4,20},{6,22},{8,24},{10,26},{12,28},{14,30},{16,0},... | collective-permute-start | bytes 454664 | tf_op jit(solution)/shard_map/ppermute | solution.py:918
  437.0 14.4 %collective-permute-start.33 = (bf16[1152,128]{1,0:T(8,128)(2,1)S(1)}, bf16[1152,128]{1,0:T(8,128)(2,1)S(1)}, u32[]{:S(2)}, u32[]{:S(2)}) collective-permute-start(bf16[1152,128]{1,0:T(8,128)(2,1)S(1)} %add_convert_fusion.9), channel_id=1, source_target_pairs={{0,16},{2,18},{4,20},{6,22},{8,24},{10,26},{12,28},{14,30},{16,0},... | collective-permute-start | bytes 884744 | tf_op jit(solution)/shard_map/ppermute | solution.py:918
  437.2 14.6 %collective-permute-start.15 = (bf16[4,16,768]{2,1,0:T(8,128)(2,1)S(1)}, bf16[4,16,768]{2,1,0:T(8,128)(2,1)S(1)}, u32[]{:S(2)}, u32[]{:S(2)}) collective-permute-start(bf16[4,16,768]{2,1,0:T(8,128)(2,1)S(1)} %constant_dynamic-slice_fusion.10), channel_id=1, source_target_pairs={{0,8},{2,10},{4,12},{6,14},{8,0},{10,2},{12,4},{14,6},{16,24},{18,... | collective-permute-start | bytes 294920 | tf_op jit(solution)/shard_map/ppermute | solution.py:808
  445.5 12.4 %collective-permute-start.24 = (bf16[1184,128]{1,0:T(8,128)(2,1)S(1)}, bf16[1184,128]{1,0:T(8,128)(2,1)S(1)}, u32[]{:S(2)}, u32[]{:S(2)}) collective-permute-start(bf16[1184,128]{1,0:T(8,128)(2,1)S(1)} %maximum_select_fusion.10), channel_id=1, source_target_pairs={{0,8},{2,10},{4,12},{6,14},{8,0},{10,2},{12,4},{14,6},{16,24},{18,... | collective-permute-start | bytes 909320 | tf_op jit(solution)/shard_map/ppermute | solution.py:918
  451.6 18.7 %collective-permute-start.34 = (bf16[2304,128]{1,0:T(8,128)(2,1)S(1)}, bf16[2304,128]{1,0:T(8,128)(2,1)S(1)}, u32[]{:S(2)}, u32[]{:S(2)}) collective-permute-start(bf16[2304,128]{1,0:T(8,128)(2,1)S(1)} %maximum_select_fusion.7), channel_id=1, source_target_pairs={{0,8},{2,10},{4,12},{6,14},{8,0},{10,2},{12,4},{14,6},{16,24},{18,... | collective-permute-start | bytes 1769480 | tf_op jit(solution)/shard_map/ppermute | solution.py:918
  451.8 20.9 %collective-permute-start.16 = (bf16[2,16,768]{2,1,0:T(8,128)(2,1)S(1)}, bf16[2,16,768]{2,1,0:T(8,128)(2,1)S(1)}, u32[]{:S(2)}, u32[]{:S(2)}) collective-permute-start(bf16[2,16,768]{2,1,0:T(8,128)(2,1)S(1)} %constant_dynamic-slice_fusion.9), channel_id=1, source_target_pairs={{0,4},{2,6},{4,0},{6,2},{8,12},{10,14},{12,8},{14,10},{16,20},{18,... | collective-permute-start | bytes 147464 | tf_op jit(solution)/shard_map/ppermute | solution.py:808
  458.1 14.6 %collective-permute-start.25 = (bf16[2368,128]{1,0:T(8,128)(2,1)S(1)}, bf16[2368,128]{1,0:T(8,128)(2,1)S(1)}, u32[]{:S(2)}, u32[]{:S(2)}) collective-permute-start(bf16[2368,128]{1,0:T(8,128)(2,1)S(1)} %maximum_select_fusion.6), channel_id=1, source_target_pairs={{0,4},{2,6},{4,0},{6,2},{8,12},{10,14},{12,8},{14,10},{16,20},{18,... | collective-permute-start | bytes 1818632 | tf_op jit(solution)/shard_map/ppermute | solution.py:918
  470.6 31.0 %collective-permute-start.35 = (bf16[4608,128]{1,0:T(8,128)(2,1)S(1)}, bf16[4608,128]{1,0:T(8,128)(2,1)}, u32[]{:S(2)}, u32[]{:S(2)}) collective-permute-start(bf16[4608,128]{1,0:T(8,128)(2,1)S(1)} %maximum_select_fusion.4), channel_id=1, source_target_pairs={{0,4},{2,6},{4,0},{6,2},{8,12},{10,14},{12,8},{14,10},{16,20},{18,... | collective-permute-start | bytes 3538952 | tf_op jit(solution)/shard_map/ppermute | solution.py:918
  474.0 37.6 %collective-permute-start.26 = (bf16[4736,128]{1,0:T(8,128)(2,1)}, bf16[4736,128]{1,0:T(8,128)(2,1)}, u32[]{:S(2)}, u32[]{:S(2)}) collective-permute-start(bf16[4736,128]{1,0:T(8,128)(2,1)} %maximum_select_fusion.3), channel_id=1, source_target_pairs={{0,2},{2,0},{4,6},{6,4},{8,10},{10,8},{12,14},{14,12},{16,18},{18,... | collective-permute-start | bytes 3637256 | tf_op jit(solution)/shard_map/ppermute | solution.py:918
  475.2 24.0 %collective-permute-start.17 = (bf16[1,16,768]{2,1,0:T(8,128)(2,1)S(1)}, bf16[1,16,768]{2,1,0:T(8,128)(2,1)S(1)}, u32[]{:S(2)}, u32[]{:S(2)}) collective-permute-start(bf16[1,16,768]{2,1,0:T(8,128)(2,1)S(1)} %get-tuple-element.177), channel_id=1, source_target_pairs={{0,2},{2,0},{4,6},{6,4},{8,10},{10,8},{12,14},{14,12},{16,18},{18,... | collective-permute-start | bytes 73736 | tf_op jit(solution)/shard_map/ppermute | solution.py:808
  511.1 32.6 %collective-permute-start.36 = (bf16[9216,128]{1,0:T(8,128)(2,1)S(1)}, bf16[9216,128]{1,0:T(8,128)(2,1)}, u32[]{:S(2)}, u32[]{:S(2)}) collective-permute-start(bf16[9216,128]{1,0:T(8,128)(2,1)S(1)} %maximum_select_fusion.2), channel_id=1, source_target_pairs={{0,2},{2,0},{4,6},{6,4},{8,10},{10,8},{12,14},{14,12},{16,18},{18,... | collective-permute-start | bytes 7077896 | tf_op jit(solution)/shard_map/ppermute | solution.py:918
  518.2 24.2 %collective-permute-start.27 = (f32[4608]{0:T(1024)}, f32[4608]{0:T(1024)}, u32[]{:S(2)}, u32[]{:S(2)}) collective-permute-start(f32[4608]{0:T(1024)} %slice_bitcast_fusion.2), channel_id=1, source_target_pairs={{0,1},{1,0},{2,3},{3,2},{4,5},{5,4},{6,7},{7,6},{8,9},{9,8},{10,11... | collective-permute-start | bytes 55304 | tf_op jit(solution)/shard_map/ppermute | solution.py:811
  (26 other events, 108.9 us)
